TPU v7x, 128 devices: a whole 4x4x4 slice. The times are simulated.
128 devices in a mesh: cache: 16 (over x, z_lo, core), head: 8 (over y, z_hi).
Axes of the slice: x: 4, y: 4, z: 4 (z_hi: 2, z_lo: 2; z = z_hi * 2 + z_lo), core: 2. Of those that a mesh axis runs over, the one named last changes fastest.
Arguments:
- hidden: bfloat16 [2, 2048, 8192], P(None, 'cache', 'head'), may hold values from -6 to 6
- norm_gain: bfloat16 [8192], replicated, may hold values from 0.25 to 1.75
- w_query: bfloat16 [8192, 4096], P(None, 'head'), may hold values from -0.109375 to 0.109375
- key_weight: bfloat16 [8192, 1024], P(None, 'head'), may hold values from -0.109375 to 0.109375
- value_weight: bfloat16 [8192, 1024], P(None, 'head'), may hold values from -0.0625 to 0.0625
- w_out: bfloat16 [4096, 8192], P('head'), may hold values from -0.09375 to 0.09375
- key_cache: bfloat16 [2048, 64, 8, 128], P('cache', None, 'head'), may hold values from -450 to 450
- value_cache: bfloat16 [2048, 64, 8, 128], P('cache', None, 'head'), may hold values from -6 to 6
- tree_pages: int32 [16, 128, 8], P('cache'), may hold values from 0 to 127
- page_fill: int32 [16, 128, 8], P('cache'), may hold values from 1 to 64, as said below
- row_depth: int32 [16, 2048], P('cache'), may hold values from 0 to 8, as said below
- row_length: int32 [2048], P('cache'), may hold values from 0 to 8192, as said below
Outputs:
- attn_out: bfloat16 [2, 2048, 8192], P(None, 'cache', 'head')
Inputs may be any that keep to these rules, and one draw needn't show every extreme that they name: `page_fill`: slot 0 of every tree on every block holds 64 tokens, and so does every slot of tree 0 on every block. `row_depth`: the first row of every tree (r % 16 == 0) has depth 8 on every block. `row_length`: equals the sum over blocks c and slots s < row_depth[c, r] of page_fill[c, r // 16, s].
All inputs are finite; a program needn't handle non-finite values.
Results may differ from a plain program's by a relative error of at most 0.012.
The roundings to bfloat16 on the way count: a program that leaves them out, or rounds other values in their place, can miss the bound.
Values may be sent and summed in bfloat16 or wider, within the bound.
A program may use at most 128 MiB of HBM per device.

v0:
```python
import math

import jax
import jax.numpy as jnp
from jax import lax
from jax.sharding import PartitionSpec as P

TREE_BRANCHES = 16


ROPE_BASE = 500000.0
EPSILON = 1e-05
LOW_SCORE = -1e30


def passed_along(shard, axis, by):
    length = lax.axis_size(axis)
    return lax.ppermute(shard, axis, [(i, (i + by) % length) for i in range(length)])


def apply_rotary(vectors, position_list):
    half_width = vectors.shape[-1] // 2
    ladder = jnp.arange(half_width, dtype=jnp.float32) * (2.0 / vectors.shape[-1])
    frequency = jnp.power(jnp.float32(ROPE_BASE), -ladder)
    angles = position_list.astype(jnp.float32)[..., None] * frequency
    cosine = jnp.cos(angles)
    sine_part = jnp.sin(angles)
    front_half = vectors[..., :half_width]
    back_half = vectors[..., half_width:]
    return jnp.concatenate(
        [front_half * cosine - back_half * sine_part, back_half * cosine + front_half * sine_part],
        axis=-1,
    )


def combine(earlier, later):
    first_max, first_total, first_out = earlier
    second_max, second_total, second_out = later
    highest = jnp.maximum(first_max, second_max)
    first_scale = jnp.exp(first_max - highest)
    second_scale = jnp.exp(second_max - highest)
    summed = first_scale * first_total + second_scale * second_total
    merged = first_scale[..., None] * first_out + second_scale[..., None] * second_out
    return (highest, summed, merged)


def body(
    hidden,
    norm_gain,
    w_query,
    key_weight,
    value_weight,
    w_out,
    key_cache,
    value_cache,
    tree_pages,
    page_fill,
    row_depth,
    row_length,
):
    members = lax.axis_size("cache")
    my_index = lax.axis_index("cache")
    positions_n = hidden.shape[0]
    local_rows = hidden.shape[1]
    page_size = key_cache.shape[1]
    kv_local = key_cache.shape[2]
    head_dim = key_cache.shape[3]
    query_local = w_query.shape[1] // head_dim
    group_width = query_local // kv_local
    tree_rows = TREE_BRANCHES
    score_scale = 1.0 / math.sqrt(head_dim)
    full_rows = lax.all_gather(hidden, "head", axis=2, tiled=True)
    widened = full_rows.astype(jnp.float32)
    mean_square = jnp.mean(widened * widened, axis=-1, keepdims=True)
    normalized_input = (
        widened * lax.rsqrt(mean_square + EPSILON) * norm_gain.astype(jnp.float32)
    ).astype(jnp.bfloat16)
    position_list = row_length[None, :] + jnp.arange(positions_n, dtype=jnp.int32)[:, None]
    query = apply_rotary(
        jnp.dot(normalized_input, w_query, preferred_element_type=jnp.float32).reshape(
            positions_n, local_rows, query_local, head_dim
        ),
        position_list[:, :, None],
    ).astype(jnp.bfloat16)
    fresh_key = apply_rotary(
        jnp.dot(normalized_input, key_weight, preferred_element_type=jnp.float32).reshape(
            positions_n, local_rows, kv_local, head_dim
        ),
        position_list[:, :, None],
    ).astype(jnp.bfloat16)
    fresh_value = (
        jnp.dot(normalized_input, value_weight, preferred_element_type=jnp.float32)
        .astype(jnp.bfloat16)
        .reshape(positions_n, local_rows, kv_local, head_dim)
    )
    travel = query.reshape(positions_n, local_rows, kv_local, group_width, head_dim).transpose(
        1, 2, 0, 3, 4
    )
    travel = travel.reshape(local_rows, kv_local, positions_n * group_width, head_dim)
    new_scores = (
        jnp.einsum("rkxd,qrkd->rkxq", travel, fresh_key, preferred_element_type=jnp.float32)
        * score_scale
    )
    query_spot = jnp.arange(positions_n * group_width) // group_width
    causal = query_spot[:, None] >= jnp.arange(positions_n)[None, :]
    new_max = jnp.max(jnp.where(causal, new_scores, LOW_SCORE), axis=-1)
    new_weights = jnp.where(causal, jnp.exp(new_scores - new_max[..., None]), 0.0).astype(
        jnp.bfloat16
    )
    new_total = jnp.sum(new_weights.astype(jnp.float32), axis=-1)
    new_out = jnp.einsum(
        "rkxq,qrkd->rkxd", new_weights, fresh_value, preferred_element_type=jnp.float32
    )

    def cache_part(query_block, first_row):
        block_rows = query_block.shape[0]
        tree_count = block_rows // tree_rows
        first_tree = first_row // tree_rows
        page_numbers = lax.dynamic_slice_in_dim(tree_pages[0], first_tree, tree_count, 0)
        page_tokens = lax.dynamic_slice_in_dim(page_fill[0], first_tree, tree_count, 0)
        depths = lax.dynamic_slice_in_dim(row_depth[0], first_row, block_rows, 0)
        key_width = page_numbers.shape[1] * page_size
        paged_keys = key_cache[page_numbers].reshape(tree_count, key_width, kv_local, head_dim)
        paged_values = value_cache[page_numbers].reshape(tree_count, key_width, kv_local, head_dim)
        grouped_queries = query_block.reshape(
            tree_count, tree_rows, kv_local, query_block.shape[2], head_dim
        )
        scores = (
            jnp.einsum(
                "trkxd,tnkd->trkxn", grouped_queries, paged_keys, preferred_element_type=jnp.float32
            )
            * score_scale
        )
        column = jnp.arange(key_width, dtype=jnp.int32)
        slot_of = column // page_size
        token_of = column % page_size
        filled = jnp.repeat(page_tokens, page_size, axis=1)
        visible = (slot_of[None, None, :] < depths.reshape(tree_count, tree_rows)[:, :, None]) & (
            token_of[None, :] < filled
        )[:, None, :]
        visible = visible[:, :, None, None, :]
        block_max = jnp.max(jnp.where(visible, scores, LOW_SCORE), axis=-1)
        weights = jnp.where(visible, jnp.exp(scores - block_max[..., None]), 0.0).astype(
            jnp.bfloat16
        )
        block_total = jnp.sum(weights.astype(jnp.float32), axis=-1)
        block_out = jnp.einsum(
            "trkxn,tnkd->trkxd", weights, paged_values, preferred_element_type=jnp.float32
        )
        width_x = query_block.shape[2]
        return (
            block_max.reshape(block_rows, kv_local, width_x),
            block_total.reshape(block_rows, kv_local, width_x),
            block_out.reshape(block_rows, kv_local, width_x, head_dim),
        )

    position_spans = [
        (which_pos * group_width, (which_pos + 1) * group_width) for which_pos in range(positions_n)
    ]
    pieces = []
    for span_low, span_high in position_spans:
        query_part = travel[:, :, span_low:span_high]
        initial = (
            new_max[:, :, span_low:span_high],
            new_total[:, :, span_low:span_high],
            new_out[:, :, span_low:span_high],
        )

        def advance(hop_index, loop_state):
            moving, carried = loop_state
            anchor = (my_index - hop_index) % members
            carried = combine(carried, cache_part(moving, anchor * local_rows))
            moving = passed_along(moving, "cache", 1)
            carried = passed_along((carried[0], carried[1], carried[2]), "cache", 1)
            return (moving, carried)

        moving, carried = lax.fori_loop(0, members - 1, advance, (query_part, initial))
        anchor = (my_index + 1) % members
        carried = combine(carried, cache_part(moving, anchor * local_rows))
        result = passed_along((carried[0], carried[1], carried[2]), "cache", 1)
        pieces.append(result[2] / result[1][..., None])
    attention = jnp.concatenate(pieces, axis=2).astype(jnp.bfloat16)
    attention = attention.reshape(
        local_rows, kv_local, positions_n, group_width, head_dim
    ).transpose(2, 0, 1, 3, 4)
    flat_attention = attention.reshape(positions_n * local_rows, query_local * head_dim)
    out_rows = w_out.shape[1] // lax.axis_size("head")
    reduced = lax.psum_scatter(
        lax.dot_general(
            w_out, flat_attention, (((0,), (1,)), ((), ())), preferred_element_type=jnp.float32
        ),
        "head",
        scatter_dimension=0,
        tiled=True,
    )
    return (
        reduced.reshape(out_rows, positions_n, local_rows).transpose(1, 2, 0).astype(jnp.bfloat16)
    )


def solution(mesh):
    in_specs = (
        P(None, "cache", "head"),
        P(),
        P(None, "head"),
        P(None, "head"),
        P(None, "head"),
        P("head", None),
        P("cache", None, "head", None),
        P("cache", None, "head", None),
        P("cache", None, None),
        P("cache", None, None),
        P("cache", None),
        P("cache"),
    )
    out_specs = P(None, "cache", "head")
    return jax.shard_map(body, mesh=mesh, in_specs=in_specs, out_specs=out_specs, check_vma=False)
```

profile of v0, /device:TPU:0, one launch (start us, length us, event | category | flops | bytes accessed | tf_op | source)
XLA Modules:
  0.0 1031.4 jit_solution(5673336819663232801)
XLA Ops:
  21.2 62.6 %all-gather.2.cloned.1.call-done = bf16[2,128,8192]{2,1,0:T(8,128)(2,1)} async-done(((bf16[2,128,1024]{2,1,0:T(8,128)(2,1)}), bf16[2,128,8192]{2,1,0:T(8,128)(2,1)}) %all-gather.2.cloned.1.call-update) | async-done | bytes 4194320 | tf_op jit(solution)/shard_map/all_gather | solution.py:72
  108.0 388.1 %while.45 = (s32[]{:T(128)}, bf16[128,1,4,128]{3,2,1,0:T(4,128)(2,1)}, f32[128,1,4]{0,2,1:T(4,128)}, f32[128,1,4]{0,2,1:T(4,128)}, f32[128,1,4,128]{3,0,2,1:T(8,...) while((s32[]{:T(128)}, ...), condition=%wide.region_12.13_spmd, body=%wide.region_9.12_spmd.sunk | while | flops 137444064 | bytes 14462723 | solution.py:177
  201.6 9.2 collective-permute-done.5
  227.5 9.2 collective-permute-done.5
  253.4 9.2 collective-permute-done.5
  279.3 9.2 collective-permute-done.5
  305.1 9.2 collective-permute-done.5
  331.0 9.2 collective-permute-done.5
  356.9 9.2 collective-permute-done.5
  382.8 9.2 collective-permute-done.5
  408.6 9.2 collective-permute-done.5
  434.5 9.2 collective-permute-done.5
  460.4 9.2 collective-permute-done.5
  486.3 9.2 collective-permute-done.5
  498.9 387.8 %while.44 = (s32[]{:T(128)}, bf16[128,1,4,128]{3,2,1,0:T(4,128)(2,1)}, f32[128,1,4]{0,2,1:T(4,128)}, f32[128,1,4]{0,2,1:T(4,128)}, f32[128,1,4,128]{3,0,2,1:T(8,...) while((s32[]{:T(128)}, ...), condition=%wide.region_6.7_spmd, body=%wide.region_3.6_spmd.sunk | while | flops 137444064 | bytes 14987039 | solution.py:177
  514.9 9.1 collective-permute-done.1
  540.7 9.1 collective-permute-done.1
  566.6 9.1 collective-permute-done.1
  592.4 9.1 collective-permute-done.1
  618.3 9.1 collective-permute-done.1
  670.0 9.1 collective-permute-done.1
  721.7 9.1 collective-permute-done.1
  893.3 10.0 collective-permute-done.11
  912.9 109.6 %reduce-scatter.2.cloned.1.call-done = f32[1024,256]{0,1:T(8,128)} async-done(((f32[8192,256]{0,1:T(8,128)}), f32[1024,256]{0,1:T(8,128)}) %reduce-scatter.2.cloned.1.call-update) | async-done | bytes 1048592 | tf_op jit(solution)/shard_map/reduce_scatter | solution.py:188
  (1318 shorter events, 658.7 us)
Async XLA Ops:
  6.5 77.3 %all-gather.2.cloned.1.call-start = ((), (), s32[]{:S(2)}) async-start(), calls=%async_computation.1 | async-start | bytes 4718592 | tf_op jit(solution)/shard_map/all_gather | solution.py:72
  7.3 1015.2 %reduce-scatter.2.cloned.1.call-start = ((), (), s32[]{:S(2)}) async-start(), calls=%async_computation.2 | async-start | bytes 9437184 | tf_op jit(solution)/shard_map/reduce_scatter | solution.py:188
  123.7 9.5 collective-permute-start.7
  149.5 9.5 collective-permute-start.7
  175.4 9.5 collective-permute-start.7
  201.3 9.5 collective-permute-start.7
  227.2 9.5 collective-permute-start.7
  253.0 9.5 collective-permute-start.7
  278.9 9.5 collective-permute-start.7
  304.8 9.5 collective-permute-start.7
  330.7 9.5 collective-permute-start.7
  356.6 9.5 collective-permute-start.7
  382.4 9.5 collective-permute-start.7
  408.3 9.5 collective-permute-start.7
  434.2 9.5 collective-permute-start.7
  460.1 9.5 collective-permute-start.7
  486.0 9.5 collective-permute-start.7
  514.6 9.4 collective-permute-start.3
  540.4 9.4 collective-permute-start.3
  566.2 9.4 collective-permute-start.3
  892.5 10.8 %collective-permute-start.10 = (f32[128,1,4,128]{3,0,2,1:T(8,128)S(1)}, f32[128,1,4,128]{3,0,2,1:T(8,128)S(1)}, u32[]{:S(2)}, u32[]{:S(2)}) collective-permute-start(f32[128,1,4,128]{3,0,2,1:T(8,128)S(1)} %fusion.58), channel_id=1, source_target_pairs={{0,8},{8,16},{16,24},{24,32},{32,40},{40,48},{48,56},{56,64},{64,7... | collective-permute-start | bytes 786440 | tf_op jit(solution)/shard_map/ppermute | solution.py:18
  892.8 10.6 %collective-permute-start.8 = (f32[128,1,4,128]{3,0,2,1:T(8,128)S(1)}, f32[128,1,4,128]{3,0,2,1:T(8,128)S(1)}, u32[]{:S(2)}, u32[]{:S(2)}) collective-permute-start(f32[128,1,4,128]{3,0,2,1:T(8,128)S(1)} %fusion.59), channel_id=1, source_target_pairs={{0,8},{8,16},{16,24},{24,32},{32,40},{40,48},{48,56},{56,64},{64,7... | collective-permute-start | bytes 786440 | tf_op jit(solution)/shard_map/ppermute | solution.py:18
  892.9 10.4 %collective-permute-start.11 = (f32[128,1,4]{0,2,1:T(4,128)S(1)}, f32[128,1,4]{0,2,1:T(4,128)S(1)}, u32[]{:S(2)}, u32[]{:S(2)}) collective-permute-start(f32[128,1,4]{0,2,1:T(4,128)S(1)} %get-tuple-element.804), channel_id=1, source_target_pairs={{0,8},{8,16},{16,24},{24,32},{32,40},{40,48},{48,56},{56,64},{64,7... | collective-permute-start | bytes 6152 | tf_op jit(solution)/shard_map/ppermute | solution.py:18
  893.0 10.5 %collective-permute-start.9 = (f32[128,1,4]{0,2,1:T(4,128)S(1)}, f32[128,1,4]{0,2,1:T(4,128)S(1)}, u32[]{:S(2)}, u32[]{:S(2)}) collective-permute-start(f32[128,1,4]{0,2,1:T(4,128)S(1)} %get-tuple-element.801), channel_id=1, source_target_pairs={{0,8},{8,16},{16,24},{24,32},{32,40},{40,48},{48,56},{56,64},{64,7... | collective-permute-start | bytes 6152 | tf_op jit(solution)/shard_map/ppermute | solution.py:18
  (219 other events, 1144.1 us)
Sparse Core Ops, SparseCore 0:
  9.7 74.0 all-gather.1
  913.0 109.4 reduce-scatter.1
where the time goes:
time: 1040 us; the launch traced here: 1030 us
  waiting for transfers between devices  452 us (43%)
  local copies, waits for them, and re-layouts  330 us (32%)
  other arithmetic  124 us (12%)
  matrix products  94.2 us (9%)
  starting transfers between devices  14.7 us (1%)
  between operations  13.9 us (1%)
    ppermute x124, waiting for transfers between devices, passed_along(): lax.ppermute(shard, axis, [(i, (i + by) % length) for i in range(length)])  279 us
    reduce_scatter x1, waiting for transfers between devices, body(): lax.psum_scatter(lax.dot_general(w_out, flat_attention, (((0,), (1,)), ((...  110 us
    gather x31, local copies, waits for them, and re-layouts, cache_part(): key_cache[page_numbers].reshape(tree_count, key_width, kv_local, head_dim)  101 us
    gather x31, local copies, waits for them, and re-layouts, cache_part(): value_cache[page_numbers].reshape(tree_count, key_width, kv_local, head_dim)  73.4 us
    all_gather x1, waiting for transfers between devices, body(): full_rows = lax.all_gather(hidden, 'head', axis=2, tiled=True)  62.6 us
    dot_general x32, matrix products, cache_part(): jnp.einsum('trkxd,tnkd->trkxn', grouped_queries, paged_keys, preferred_el...  58.9 us
    add x32, other arithmetic, combine(): first_scale[..., None] * first_out + second_scale[..., None] * second_out  35.3 us
    another operation x30, local copies, waits for them, and re-layouts  27.3 us
  transfers between devices with their start and end apart: 126, of which 33 were waited for; matrix products, arithmetic and copies ran while one was open for 1% of the time, Pallas kernels for 0%

commit v1 on v0

v1 whole, which is shorter than its diff:
```python
import math

import jax
import jax.numpy as jnp
from jax import lax
from jax.experimental import pallas as pl
from jax.experimental.pallas import tpu as pltpu
from jax.sharding import PartitionSpec as P

ROPE_BASE = 500000.0
EPSILON = 1e-05


def apply_rotary(vectors, position_list):
    half_width = vectors.shape[-1] // 2
    ladder = jnp.arange(half_width, dtype=jnp.float32) * (2.0 / vectors.shape[-1])
    frequency = jnp.power(jnp.float32(ROPE_BASE), -ladder)
    angles = position_list.astype(jnp.float32)[..., None] * frequency
    cosine = jnp.cos(angles)
    sine_part = jnp.sin(angles)
    front_half = vectors[..., :half_width]
    back_half = vectors[..., half_width:]
    return jnp.concatenate(
        [front_half * cosine - back_half * sine_part, back_half * cosine + front_half * sine_part],
        axis=-1,
    )


MESH = pl.DeviceIdType.MESH
LOW_SCORE = -1e30
LOW_MAX = -1e29
EXP_SCALE = math.log2(math.e) / math.sqrt(128.0)


def place():
    c = lax.axis_index("cache")
    h = lax.axis_index("head")
    return c // 4, lax.rem(c // 2, 2), lax.rem(c, 2), h


def attention_kernel(
    pages, q_own, key_new, value_new, lim, keys, values,
    out,
    q_all, part, part_stat, got, got_stat, relay, relay_stat, rowed, rowed_stat, fresh, fresh_stat,
    lhs, send_sem, recv_sem,
):
    x, zl, core, h = place()

    def at(dx, dz):
        return (lax.rem(x + dx, 4) * 4 + (zl if dz == 0 else 1 - zl) * 2 + core, h)

    ahead, behind, across = at(1, 0), at(3, 0), at(0, 1)
    barrier = pltpu.get_barrier_semaphore()
    for device in (ahead, behind, across):
        pl.semaphore_signal(barrier, inc=1, device_id=device, device_id_type=MESH)
    pl.semaphore_wait(barrier, 3)

    made = {}

    def send(name, src, dst, device):
        number = len(made)
        copy = pltpu.make_async_remote_copy(
            src_ref=src, dst_ref=dst, send_sem=send_sem.at[number], recv_sem=recv_sem.at[number],
            device_id=device, device_id_type=MESH,
        )
        made[name] = copy
        copy.start()

    def arrived(*names):
        for name in names:
            made[name].wait_recv()

    lhs[128:144, :] = jnp.ones((16, 1024), jnp.bfloat16)
    token = lax.broadcasted_iota(jnp.int32, (1024, 128), 0) % 64
    low_lanes = lax.broadcasted_iota(jnp.int32, (128, 128), 1) < 64

    def block(dx, dz):
        owner = lax.rem(x + dx, 4) * 2 + (zl if dz == 0 else 1 - zl)

        def half_loop(half):
            def tree_step(u, _):
                tree = half * 4 + u
                base = (owner * 8 + tree) * 16
                numbers = [pages[base + i] for i in range(16)]
                k = jnp.concatenate([keys[n] for n in numbers], axis=0)
                q = q_all[dx, dz, half, u]
                s = lax.dot_general(k, q, (((1,), (1,)), ((), ())), preferred_element_type=jnp.float32)
                limits = lim[owner, tree]
                limits = jnp.concatenate(
                    [jnp.broadcast_to(limits[i : i + 1], (64, 128)) for i in range(16)], axis=0
                )
                s = jnp.where(token < limits, s, LOW_SCORE)
                m = jnp.maximum(jnp.max(s, axis=0, keepdims=True), LOW_MAX)
                p = jnp.exp2((s - m) * EXP_SCALE).astype(jnp.bfloat16)
                for i in range(8):
                    lhs[0:128, i * 128 : (i + 1) * 128] = jnp.where(
                        low_lanes, values[numbers[2 * i]], values[numbers[2 * i + 1]]
                    )
                o = jnp.dot(lhs[...], p, preferred_element_type=jnp.float32)
                part[dx, dz, half, u] = o[0:128].astype(jnp.bfloat16)
                part_stat[dx, dz, half, pl.ds(u, 1), :] = m
                part_stat[dx, dz, half, pl.ds(u + 4, 1), :] = o[128:129]
                return 0

            lax.fori_loop(0, 4, tree_step, 0)

        for half in (0, 1):
            half_loop(half)
            if dx in (1, 3):
                to, slot = (ahead, 0) if dx == 1 else (behind, 1)
                send(f"o{dx}{dz}{half}", part.at[dx, dz, half], got.at[slot, dz, half], to)
                send(f"s{dx}{dz}{half}", part_stat.at[dx, dz, half], got_stat.at[slot, dz, half], to)
            if dx == 2:
                to = ahead if half == 0 else behind
                send(f"o2{dz}{half}", part.at[dx, dz, half], relay.at[dz, half], to)
                send(f"s2{dz}{half}", part_stat.at[dx, dz, half], relay_stat.at[dz, half], to)

    def pass_on(dz):
        for half in (0, 1):
            to = ahead if half == 0 else behind
            arrived(f"o2{dz}{half}", f"s2{dz}{half}")
            send(f"or{dz}{half}", relay.at[dz, half], got.at[2, dz, half], to)
            send(f"sr{dz}{half}", relay_stat.at[dz, half], got_stat.at[2, dz, half], to)

    def merged(pieces, u):
        tops = [stat[pl.ds(u, 1), :] for _, stat in pieces]
        top = tops[0]
        for other in tops[1:]:
            top = jnp.maximum(top, other)
        total = jnp.zeros((1, 128), jnp.float32)
        sums = jnp.zeros((128, 128), jnp.float32)
        for (o, stat), m in zip(pieces, tops):
            w = jnp.exp2((m - top) * EXP_SCALE)
            total += w * stat[pl.ds(u + 4, 1), :]
            sums += w * o[u].astype(jnp.float32)
        return top, total, sums

    q_all[0, 0] = q_own[...]
    send("q30", q_all.at[0, 0], q_all.at[3, 0], ahead)
    send("q10", q_all.at[0, 0], q_all.at[1, 0], behind)
    send("q01", q_all.at[0, 0], q_all.at[0, 1], across)

    spot_k = lax.broadcasted_iota(jnp.int32, (32, 128), 0)
    spot_q = lax.broadcasted_iota(jnp.int32, (32, 128), 1)
    seen = (spot_k % 16 == spot_q % 16) & (spot_k // 16 <= spot_q // 64)
    for half in (0, 1):
        def new_step(u, _):
            q = q_all[0, 0, half, u]
            s = lax.dot_general(
                key_new[half * 4 + u], q, (((1,), (1,)), ((), ())), preferred_element_type=jnp.float32
            )
            s = jnp.where(seen, s, LOW_SCORE)
            m = jnp.max(s, axis=0, keepdims=True)
            p = jnp.exp2((s - m) * EXP_SCALE).astype(jnp.bfloat16)
            o = lax.dot_general(
                value_new[half * 4 + u], p, (((0,), (0,)), ((), ())), preferred_element_type=jnp.float32
            )
            fresh[half, u] = o.astype(jnp.bfloat16)
            fresh_stat[half, pl.ds(u, 1), :] = m
            fresh_stat[half, pl.ds(u + 4, 1), :] = jnp.sum(p.astype(jnp.float32), axis=0, keepdims=True)
            return 0

        lax.fori_loop(0, 4, new_step, 0)

    block(0, 0)
    arrived("q30")
    send("q20a", q_all.at[3, 0, 0], q_all.at[2, 0, 0], ahead)
    arrived("q10")
    send("q20b", q_all.at[1, 0, 1], q_all.at[2, 0, 1], behind)
    arrived("q01")
    send("q31", q_all.at[0, 1], q_all.at[3, 1], ahead)
    send("q11", q_all.at[0, 1], q_all.at[1, 1], behind)
    block(1, 0)
    block(3, 0)
    arrived("q20a")
    send("q21a", q_all.at[2, 0, 0], q_all.at[2, 1, 0], across)
    arrived("q20b")
    send("q21b", q_all.at[2, 0, 1], q_all.at[2, 1, 1], across)
    block(2, 0)
    arrived("q11", "q31")
    block(1, 1)
    block(3, 1)
    pass_on(0)
    arrived("q21a", "q21b")
    block(2, 1)
    block(0, 1)
    pass_on(1)
    for half in (0, 1):
        arrived(*[f"{a}{b}1{half}" for a in "os" for b in (1, 3)], f"or1{half}", f"sr1{half}")
        pieces = [(part.at[0, 1, half], part_stat.at[0, 1, half])]
        pieces += [(got.at[i, 1, half], got_stat.at[i, 1, half]) for i in range(3)]

        def row_step(u, _):
            top, total, sums = merged(pieces, u)
            rowed[0, half, u] = sums.astype(jnp.bfloat16)
            rowed_stat[0, half, pl.ds(u, 1), :] = top
            rowed_stat[0, half, pl.ds(u + 4, 1), :] = total
            return 0

        lax.fori_loop(0, 4, row_step, 0)
        send(f"oz{half}", rowed.at[0, half], rowed.at[1, half], across)
        send(f"sz{half}", rowed_stat.at[0, half], rowed_stat.at[1, half], across)
    for half in (0, 1):
        arrived(*[f"{a}{b}0{half}" for a in "os" for b in (1, 3)], f"or0{half}", f"sr0{half}")
        arrived(f"oz{half}", f"sz{half}")
        pieces = [(part.at[0, 0, half], part_stat.at[0, 0, half])]
        pieces += [(got.at[i, 0, half], got_stat.at[i, 0, half]) for i in range(3)]
        pieces += [(rowed.at[1, half], rowed_stat.at[1, half]), (fresh.at[half], fresh_stat.at[half])]

        def last_step(u, _):
            top, total, sums = merged(pieces, u)
            out[half * 4 + u] = jnp.transpose(sums / total).astype(jnp.bfloat16)
            return 0

        lax.fori_loop(0, 4, last_step, 0)
    for copy in made.values():
        copy.wait_send()


def attention_call(pages, q_own, key_new, value_new, lim, keys, values):
    blk = (2, 4, 128, 128)
    st = (2, 8, 128)
    bf, f32 = jnp.bfloat16, jnp.float32
    vm = pl.BlockSpec(memory_space=pltpu.VMEM)
    return pl.pallas_call(
        attention_kernel,
        out_shape=jax.ShapeDtypeStruct((8, 128, 128), bf),
        in_specs=[pl.BlockSpec(memory_space=pltpu.SMEM)] + [vm] * 6,
        out_specs=vm,
        scratch_shapes=[
            pltpu.VMEM((4, 2) + blk, bf),
            pltpu.VMEM((4, 2) + blk, bf),
            pltpu.VMEM((4, 2) + st, f32),
            pltpu.VMEM((3, 2) + blk, bf),
            pltpu.VMEM((3, 2) + st, f32),
            pltpu.VMEM((2,) + blk, bf),
            pltpu.VMEM((2,) + st, f32),
            pltpu.VMEM((2,) + blk, bf),
            pltpu.VMEM((2,) + st, f32),
            pltpu.VMEM(blk, bf),
            pltpu.VMEM(st, f32),
            pltpu.VMEM((144, 1024), bf),
            pltpu.SemaphoreType.DMA((48,)),
            pltpu.SemaphoreType.DMA((48,)),
        ],
        compiler_params=pltpu.CompilerParams(
            collective_id=2, has_side_effects=True, vmem_limit_bytes=50 * 2**20
        ),
        cost_estimate=pl.CostEstimate(flops=9 * 10**9, bytes_accessed=16 * 2**20, transcendentals=10**7),
    )(pages, q_own.reshape((2, 4, 128, 128)), key_new, value_new, lim, keys, values)


def sibling(array):
    return lax.ppermute(array, "cache", [(i, i ^ 1) for i in range(16)])


def tables(tree_pages, page_fill, row_depth):
    core = lax.rem(lax.axis_index("cache"), 2)
    pages = tree_pages[0].reshape(8, 2, 8, 8)
    fill = page_fill[0].reshape(8, 2, 8, 8)
    depth = row_depth[0].reshape(8, 2, 8, 16)
    packed = jnp.concatenate([pages, fill, depth], axis=-1)
    mine = lax.dynamic_index_in_dim(packed, core, 1, keepdims=False)
    theirs = sibling(lax.dynamic_index_in_dim(packed, 1 - core, 1, keepdims=False))

    def limits(t):
        lanes = jnp.tile(t[..., None, 16:32], (1, 1, 1, 8))
        slot = jnp.arange(8, dtype=jnp.int32)[:, None]
        return jnp.where(slot < lanes, t[..., 8:16, None], 0)

    numbers = jnp.concatenate([mine[..., :8], theirs[..., :8] + 128], axis=-1)
    lim = jnp.concatenate([limits(mine), limits(theirs)], axis=2)
    return numbers.reshape(-1), lim


def body(
    hidden,
    norm_gain,
    w_query,
    key_weight,
    value_weight,
    w_out,
    key_cache,
    value_cache,
    tree_pages,
    page_fill,
    row_depth,
    row_length,
):
    positions_n = hidden.shape[0]
    local_rows = hidden.shape[1]
    page_size = key_cache.shape[1]
    kv_local = key_cache.shape[2]
    head_dim = key_cache.shape[3]
    query_local = w_query.shape[1] // head_dim
    full_rows = lax.all_gather(hidden, "head", axis=2, tiled=True)
    widened = full_rows.astype(jnp.float32)
    mean_square = jnp.mean(widened * widened, axis=-1, keepdims=True)
    normalized_input = (
        widened * lax.rsqrt(mean_square + EPSILON) * norm_gain.astype(jnp.float32)
    ).astype(jnp.bfloat16)
    position_list = row_length[None, :] + jnp.arange(positions_n, dtype=jnp.int32)[:, None]
    query = apply_rotary(
        jnp.dot(normalized_input, w_query, preferred_element_type=jnp.float32).reshape(
            positions_n, local_rows, query_local, head_dim
        ),
        position_list[:, :, None],
    ).astype(jnp.bfloat16)
    fresh_key = apply_rotary(
        jnp.dot(normalized_input, key_weight, preferred_element_type=jnp.float32).reshape(
            positions_n, local_rows, kv_local, head_dim
        ),
        position_list[:, :, None],
    ).astype(jnp.bfloat16)
    fresh_value = (
        jnp.dot(normalized_input, value_weight, preferred_element_type=jnp.float32)
        .astype(jnp.bfloat16)
        .reshape(positions_n, local_rows, kv_local, head_dim)
    )
    trees = local_rows // 16
    own = query.reshape(positions_n, trees, 16, query_local, head_dim).transpose(1, 0, 3, 2, 4)
    own = own.reshape(trees, 128, head_dim)
    new_k = fresh_key.reshape(positions_n, trees, 16, head_dim).transpose(1, 0, 2, 3).reshape(trees, 32, head_dim)
    new_v = fresh_value.reshape(positions_n, trees, 16, head_dim).transpose(1, 0, 2, 3).reshape(trees, 32, head_dim)
    keys = key_cache.reshape(128, page_size, head_dim)
    values = jnp.transpose(value_cache.reshape(128, page_size, head_dim), (0, 2, 1))
    keys = jnp.concatenate([keys, sibling(keys)], axis=0)
    values = jnp.concatenate([values, sibling(values)], axis=0)
    values = jnp.concatenate([values, values], axis=2)
    numbers, lim = tables(tree_pages, page_fill, row_depth)
    attention = attention_call(numbers, own, new_k, new_v, lim, keys, values)
    attention = attention.reshape(trees, positions_n, query_local, 16, head_dim).transpose(1, 0, 3, 2, 4)
    flat_attention = attention.reshape(positions_n * local_rows, query_local * head_dim)
    out_rows = w_out.shape[1] // lax.axis_size("head")
    reduced = lax.psum_scatter(
        lax.dot_general(
            w_out, flat_attention, (((0,), (1,)), ((), ())), preferred_element_type=jnp.float32
        ),
        "head",
        scatter_dimension=0,
        tiled=True,
    )
    return (
        reduced.reshape(out_rows, positions_n, local_rows).transpose(1, 2, 0).astype(jnp.bfloat16)
    )


def solution(mesh):
    in_specs = (
        P(None, "cache", "head"),
        P(),
        P(None, "head"),
        P(None, "head"),
        P(None, "head"),
        P("head", None),
        P("cache", None, "head", None),
        P("cache", None, "head", None),
        P("cache", None, None),
        P("cache", None, None),
        P("cache", None),
        P("cache"),
    )
    out_specs = P(None, "cache", "head")
    return jax.shard_map(body, mesh=mesh, in_specs=in_specs, out_specs=out_specs, check_vma=False)
```

time: 1040 us -> 286 us (0.28)
  local copies, waits for them, and re-layouts: 330 us -> 14.8 us
  waiting for transfers between devices: 452 us -> 158 us
  other arithmetic: 124 us -> 21.6 us
  matrix products: 94.2 us -> 13.6 us
  Pallas kernels: 0 us -> 62.3 us
  starting transfers between devices: 14.7 us -> 0.8 us
    ppermute x124 -> x3, waiting for transfers between devices: 279 us -> 0.01 us  [sibling(): return lax.ppermute(array, 'cache', [(i, i ^ 1) for i in range(16)])]
    gather x62 -> x0, local copies, waits for them, and re-layouts: 174 us -> none  [the longest x31 101 us: cache_part(): key_cache[page_numbers].reshape(tree_count, key_width, kv_local, head_dim)]
    dot_general x66 -> x0, matrix products: 72.2 us -> none  [the longest x32 58.9 us: cache_part(): jnp.einsum('trkxd,tnkd->trkxn', grouped_queries, paged_keys, preferred_el...]
    pallas_call x0 -> x1, Pallas kernels: none -> 62.3 us  [attention_call(): pl.pallas_call(attention_kernel, out_shape=jax.ShapeDtypeStruct((8, 128,...]
    dynamic_slice x62 -> x0, local copies, waits for them, and re-layouts: 42.8 us -> none  [the longest x31 22 us: cache_part(): lax.dynamic_slice_in_dim(page_fill[0], first_tree, tree_count, 0)]
    mul x60 -> x0, other arithmetic: 41 us -> none  [the longest x30 20.6 us: combine(): second_scale[..., None] * second_out]
    add x34 -> x0, other arithmetic: 35.3 us -> none  [the longest x32 35.3 us: combine(): first_scale[..., None] * first_out + second_scale[..., None] * second_out]
    reshape x95 -> x2, local copies, waits for them, and re-layouts: 29 us -> 0.19 us  [the longest x1 0.11 us: body(): attention.reshape(trees, positions_n, query_local, 16, head_dim)]
  transfers between devices with their start and end apart: 126 -> 5, of which waited for: 33 -> 2; matrix products, arithmetic and copies ran while one was open for 1% -> 10% of each run, Pallas kernels for 0% -> 0%
where the time goes in v1:
time: 286 us; the launch traced here: 285 us
  waiting for transfers between devices  158 us (55%)
  Pallas kernels  62.3 us (22%)
  other arithmetic  21.6 us (8%)
  local copies, waits for them, and re-layouts  14.8 us (5%)
  between operations  13.7 us (5%)
  matrix products  13.6 us (5%)
    reduce_scatter x1, waiting for transfers between devices, body(): lax.psum_scatter(lax.dot_general(w_out, flat_attention, (((0,), (1,)), ((...  111 us
    pallas_call x1, Pallas kernels, attention_call(): pl.pallas_call(attention_kernel, out_shape=jax.ShapeDtypeStruct((8, 128,...  62.3 us
    all_gather x1, waiting for transfers between devices, body(): full_rows = lax.all_gather(hidden, 'head', axis=2, tiled=True)  46.3 us
    concatenate x1, other arithmetic, body(): values = jnp.concatenate([values, values], axis=2)  6.87 us
    unnamed x22, local copies, waits for them, and re-layouts  6.78 us
  transfers between devices with their start and end apart: 5, of which 2 were waited for; matrix products, arithmetic and copies ran while one was open for 10% of the time, Pallas kernels for 0%

profile of v1, /device:TPU:0, one launch (start us, length us, event | category | flops | bytes accessed | tf_op | source)
XLA Modules:
  0.0 285.1 jit_solution(5272670185969436842)
XLA Ops:
  6.5 0.7 all-gather.2.cloned.1.call-update
  7.4 0.5 collective-permute-start.1
  7.9 0.5 broadcast.88
  8.4 1.4 reduce.3
  9.9 0.8 copy.47
  10.6 0.8 copy.48
  11.8 0.7 add_convert_fusion.1
  12.4 0.5 multiply_cosine_fusion
  13.1 4.9 %copy.42 = bf16[128,64,1,128]{1,3,0,2:T(8,128)(2,1)} copy(bf16[128,64,1,128]{3,1,2,0:T(8,128)(2,1)} %param.19) | data formatting | bytes 4194304 | tf_op args[7]
  18.0 0.7 convert_element_type.38
  19.6 4.8 %copy.44 = bf16[128,128,64]{2,1,0:T(8,128)(2,1)} copy(bf16[128,128,64]{1,2,0:T(8,128)(2,1)} %collective-permute-done.2) | data formatting | bytes 4194304 | tf_op jit(solution)/shard_map/ppermute | solution.py:254
  24.4 4.9 %pad_maximum_fusion.keys = bf16[256,64,128]{2,1,0:T(8,128)(2,1)} fusion(bf16[128,64,128]{2,1,0:T(8,128)(2,1)} %collective-permute-done.1, bf16[128,64,128]{2,1,0:T(8,128)(2,1)} %bitcast.66), kind=kLoop, calls=%fused_computation.9 | loop fusion | flops 2097152 | bytes 8388608 | tf_op jit(solution)/shard_map/concatenate | solution.py:327
  29.3 1.4 copy-done.3
  30.7 6.9 %maximum_maximum_fusion.values = bf16[256,128,128]{2,1,0:T(8,128)(2,1)} fusion(bf16[128,128,64]{2,1,0:T(8,128)(2,1)S(1)} %copy-done.3, bf16[128,128,64]{2,1,0:T(8,128)(2,1)S(1)} %bitcast.61), kind=kLoop, calls=%fused_computation.6 | loop fusion | flops 33554432 | bytes 12582912 | tf_op jit(solution)/shard_map/concatenate | solution.py:329
  37.6 46.3 %all-gather.2.cloned.1.call-done = bf16[2,128,8192]{2,1,0:T(8,128)(2,1)} async-done(((bf16[2,128,1024]{2,1,0:T(8,128)(2,1)}), bf16[2,128,8192]{2,1,0:T(8,128)(2,1)}) %all-gather.2.cloned.1.call-update) | async-done | bytes 4194320 | tf_op jit(solution)/shard_map/all_gather | solution.py:296
  83.8 3.3 %fusion = f32[2,128]{1,0:T(2,128)S(1)} fusion(bf16[2,128,8192]{2,1,0:T(8,128)(2,1)} %all-gather.2.cloned.1.call-done), kind=kLoop, calls=%fused_computation.3 | loop fusion | flops 6291200 | bytes 4195328 | tf_op jit(solution)/shard_map/reduce_sum | solution.py:298
  87.1 3.8 %fusion.17 = bf16[2,128,128]{2,1,0:T(8,128)(2,1)S(1)} fusion(bf16[8192,128]{1,0:T(8,128)(2,1)S(1)} %copy-done, bf16[2,128,8192]{2,1,0:T(8,128)(2,1)} %all-gather.2.cloned.1.call-done, f32[8192]{0:T(1024)S(1)} %convert_element_type.38, f32[2,128]{1,0:T(2,128)S(1)} %add_rsqrt_fusion), kind=kOutput, calls=%fused_computation.15 | convolution fusion | flops 545292288 | bytes 6390784 | tf_op jit(solution)/shard_map/dot_general | solution.py:316
  90.9 1.7 fusion.12
  93.0 2.4 fusion.3
  96.0 0.3 fusion.34
  96.7 62.3 %shard_map.118 = bf16[8,128,128]{2,1,0:T(8,128)(2,1)S(1)} custom-call(s32[1024]{0:T(1024)S(1)} %reshape.117.pages, bf16[2,4,128,128]{3,2,1,0:T(8,128)(2,1)S(1)} %bitcast.57, bf16[8,32,128]{2,1,0:T(8,128)(2,1)S(1)} %bitcast.60, bf16[8,32,128]{2,1,0:T(8,128)(2,1)S(1)} %bitcast.59, s32[8,8,16,128]{3,2,1,0:T(8,128)S(1)} %pad_add_fusion.lim, ...), custom_call_target="tpu_custom_call" | custom-call | flops 8999999488 | bytes 16777216 | tf_op jit(solution)/shard_map/pallas_call | solution.py:225
  159.2 5.6 %convolution_bitcast_fusion = f32[8192,256]{0,1:T(8,128)} fusion(bf16[512,8192]{1,0:T(8,128)(2,1)S(1)} %bitcast.63, bf16[32,8,4,128]{3,2,1,0:T(4,128)(2,1)S(1)} %bitcast.67), kind=kOutput, calls=%fused_computation | convolution fusion | flops 2147483648 | bytes 17039360 | tf_op jit(solution)/shard_map/dot_general | solution.py:336
  164.8 111.3 %reduce-scatter.2.cloned.1.call-done = f32[1024,256]{0,1:T(8,128)} async-done(((f32[8192,256]{0,1:T(8,128)}), f32[1024,256]{0,1:T(8,128)}) %reduce-scatter.2.cloned.1.call-update) | async-done | bytes 1048592 | tf_op jit(solution)/shard_map/reduce_scatter | solution.py:335
  276.2 2.1 convert_element_type.42
  (57 shorter events, 2.9 us)
Async XLA Ops:
  6.5 80.6 %copy-start = (bf16[8192,128]{1,0:T(8,128)(2,1)S(1)}, bf16[8192,128]{1,0:T(8,128)(2,1)}, u32[]{:S(2)}) copy-start(bf16[8192,128]{1,0:T(8,128)(2,1)} %param.16) | copy-start | bytes 6291460
  6.5 77.3 %all-gather.2.cloned.1.call-start = ((), (), s32[]{:S(2)}) async-start(), calls=%async_computation.1 | async-start | bytes 4718592 | tf_op jit(solution)/shard_map/all_gather | solution.py:296
  7.3 268.9 %reduce-scatter.2.cloned.1.call-start = ((), (), s32[]{:S(2)}) async-start(), calls=%async_computation.2 | async-start | bytes 9437184 | tf_op jit(solution)/shard_map/reduce_scatter | solution.py:335
  7.3 12.3 %collective-permute-start.2 = (bf16[128,128,64]{1,2,0:T(8,128)(2,1)}, bf16[128,128,64]{1,2,0:T(8,128)(2,1)}, u32[]{:S(2)}, u32[]{:S(2)}) collective-permute-start(bf16[128,128,64]{1,2,0:T(8,128)(2,1)} %bitcast.64), channel_id=1, source_target_pairs={{0,8},{8,0},{16,24},{24,16},{32,40},{40,32},{48,56},{56,48},{64,72... | collective-permute-start | bytes 6291464 | tf_op jit(solution)/shard_map/ppermute | solution.py:254
  7.4 17.0 %collective-permute-start.1 = (bf16[128,64,128]{2,1,0:T(8,128)(2,1)}, bf16[128,64,128]{2,1,0:T(8,128)(2,1)}, u32[]{:S(2)}, u32[]{:S(2)}) collective-permute-start(bf16[128,64,128]{2,1,0:T(8,128)(2,1)} %bitcast.65), channel_id=1, source_target_pairs={{0,8},{8,0},{16,24},{24,16},{32,40},{40,32},{48,56},{56,48},{64,72... | collective-permute-start | bytes 6291464 | tf_op jit(solution)/shard_map/ppermute | solution.py:254
  11.6 7.3 %collective-permute-start = (s32[8,8,32]{2,1,0:T(8,128)S(1)}, s32[8,8,32]{2,1,0:T(8,128)S(1)}, u32[]{:S(2)}, u32[]{:S(2)}) collective-permute-start(s32[8,8,32]{2,1,0:T(8,128)S(1)} %get-tuple-element.12), channel_id=1, source_target_pairs={{0,8},{8,0},{16,24},{24,16},{32,40},{40,32},{48,56},{56,48},{64,72... | collective-permute-start | bytes 24584 | tf_op jit(solution)/shard_map/ppermute | solution.py:254
  24.4 4.9 %copy-start.2 = (bf16[128,64,1,128]{1,3,0,2:T(8,128)(2,1)S(1)}, bf16[128,64,1,128]{1,3,0,2:T(8,128)(2,1)}, u32[]{:S(2)}) copy-start(bf16[128,64,1,128]{1,3,0,2:T(8,128)(2,1)} %copy.42) | copy-start | bytes 6291460
  24.4 6.2 %copy-start.3 = (bf16[128,128,64]{2,1,0:T(8,128)(2,1)S(1)}, bf16[128,128,64]{2,1,0:T(8,128)(2,1)}, u32[]{:S(2)}) copy-start(bf16[128,128,64]{2,1,0:T(8,128)(2,1)} %copy.44) | copy-start | bytes 6291460
  83.8 7.1 %copy-start.4 = (bf16[2,128,8192]{2,1,0:T(8,128)(2,1)S(1)}, bf16[2,128,8192]{2,1,0:T(8,128)(2,1)}, u32[]{:S(2)}) copy-start(bf16[2,128,8192]{2,1,0:T(8,128)(2,1)} %all-gather.2.cloned.1.call-done) | copy-start | bytes 12582916
  83.8 7.1 %copy-start.5 = (bf16[8192,128]{1,0:T(8,128)(2,1)S(1)}, bf16[8192,128]{1,0:T(8,128)(2,1)}, u32[]{:S(2)}) copy-start(bf16[8192,128]{1,0:T(8,128)(2,1)} %param.15) | copy-start | bytes 6291460
  87.1 5.9 %slice-start.2 = ((s8[8388608]{0:T(1024)(128)(4,1)}), s8[4194304]{0:T(1024)(128)(4,1)S(1)}, s32[]{:S(2)}) async-start(s8[8388608]{0:T(1024)(128)(4,1)} %bitcast.75), calls=%async_computation.5 | async-start | bytes 8388608
  87.1 5.9 %slice-start.3 = ((s8[8388608]{0:T(1024)(128)(4,1)}), s8[4194304]{0:T(1024)(128)(4,1)S(1)}, s32[]{:S(2)}) async-start(s8[8388608]{0:T(1024)(128)(4,1)} %bitcast.75), calls=%async_computation.6 | async-start | bytes 8388608
  96.5 62.6 %slice-start = ((s8[8388608]{0:T(1024)(128)(4,1)}), s8[4194304]{0:T(1024)(128)(4,1)S(1)}, s32[]{:S(2)}) async-start(s8[8388608]{0:T(1024)(128)(4,1)} %bitcast.62), calls=%async_computation.3 | async-start | bytes 8388608
  96.7 62.5 %slice-start.1 = ((s8[8388608]{0:T(1024)(128)(4,1)}), s8[4194304]{0:T(1024)(128)(4,1)S(1)}, s32[]{:S(2)}) async-start(s8[8388608]{0:T(1024)(128)(4,1)} %bitcast.62), calls=%async_computation.4 | async-start | bytes 8388608
  159.2 119.1 %copy-start.1 = (bf16[8192,128]{1,0:T(8,128)(2,1)S(1)}, bf16[8192,128]{1,0:T(8,128)(2,1)}, u32[]{:S(2)}) copy-start(bf16[8192,128]{1,0:T(8,128)(2,1)} %param.16) | copy-start | bytes 6291460
Sparse Core Ops, SparseCore 0:
  9.7 74.0 all-gather.1
  165.0 111.1 reduce-scatter.1

commit v2 on v1

--- a/solution.py
+++ b/solution.py
@@ -7,26 +7,10 @@
 from jax.experimental.pallas import tpu as pltpu
 from jax.sharding import PartitionSpec as P
 
+
+MESH = pl.DeviceIdType.MESH
 ROPE_BASE = 500000.0
 EPSILON = 1e-05
-
-
-def apply_rotary(vectors, position_list):
-    half_width = vectors.shape[-1] // 2
-    ladder = jnp.arange(half_width, dtype=jnp.float32) * (2.0 / vectors.shape[-1])
-    frequency = jnp.power(jnp.float32(ROPE_BASE), -ladder)
-    angles = position_list.astype(jnp.float32)[..., None] * frequency
-    cosine = jnp.cos(angles)
-    sine_part = jnp.sin(angles)
-    front_half = vectors[..., :half_width]
-    back_half = vectors[..., half_width:]
-    return jnp.concatenate(
-        [front_half * cosine - back_half * sine_part, back_half * cosine + front_half * sine_part],
-        axis=-1,
-    )
-
-
-MESH = pl.DeviceIdType.MESH
 LOW_SCORE = -1e30
 LOW_MAX = -1e29
 EXP_SCALE = math.log2(math.e) / math.sqrt(128.0)
@@ -38,23 +22,12 @@
     return c // 4, lax.rem(c // 2, 2), lax.rem(c, 2), h
 
 
-def attention_kernel(
-    pages, q_own, key_new, value_new, lim, keys, values,
-    out,
-    q_all, part, part_stat, got, got_stat, relay, relay_stat, rowed, rowed_stat, fresh, fresh_stat,
-    lhs, send_sem, recv_sem,
-):
-    x, zl, core, h = place()
-
-    def at(dx, dz):
-        return (lax.rem(x + dx, 4) * 4 + (zl if dz == 0 else 1 - zl) * 2 + core, h)
-
-    ahead, behind, across = at(1, 0), at(3, 0), at(0, 1)
-    barrier = pltpu.get_barrier_semaphore()
-    for device in (ahead, behind, across):
-        pl.semaphore_signal(barrier, inc=1, device_id=device, device_id_type=MESH)
-    pl.semaphore_wait(barrier, 3)
-
+def column_place():
+    h = lax.axis_index("head")
+    return lax.axis_index("cache"), h // 2, lax.rem(h, 2)
+
+
+def sender(send_sem, recv_sem):
     made = {}
 
     def send(name, src, dst, device):
@@ -70,6 +43,196 @@
         for name in names:
             made[name].wait_recv()
 
+    return made, send, arrived
+
+
+def project_kernel(
+    hidden, gain, cosine, sine, w_query, key_weight, value_weight,
+    query, key_new, value_new,
+    held, stat, weight, total, send_sem, recv_sem, weight_sem,
+):
+    c, y, zh = column_place()
+    me = y * 2 + zh
+
+    def at(dy, dz):
+        return (c, lax.rem(y + dy, 4) * 2 + (zh if dz == 0 else 1 - zh))
+
+    spots = [(dy, dz) for dy in range(4) for dz in range(2)]
+    order = [(0, 0), (1, 0), (3, 0), (0, 1), (2, 0), (1, 1), (3, 1), (2, 1)]
+    loads = {}
+    for number, (dy, dz) in enumerate(order):
+        rows = pl.ds(pl.multiple_of(at(dy, dz)[1] * 1024, 1024), 1024)
+        for part, (array, low, width) in enumerate(
+            ((w_query, 0, 512), (key_weight, 512, 128), (value_weight, 640, 128))
+        ):
+            load = pltpu.make_async_copy(
+                array.at[rows], weight.at[number, :, pl.ds(low, width)], weight_sem.at[number * 3 + part]
+            )
+            load.start()
+            loads[number, part] = load
+    barrier = pltpu.get_barrier_semaphore()
+    for spot in spots[1:]:
+        pl.semaphore_signal(barrier, inc=1, device_id=at(*spot), device_id_type=MESH)
+    pl.semaphore_wait(barrier, 7)
+    made, send, arrived = sender(send_sem, recv_sem)
+    ahead, behind, across = at(1, 0), at(3, 0), at(0, 1)
+
+    for p in range(2):
+        send(f"{p}30", hidden.at[p], held.at[p, 3, 0], ahead)
+        send(f"{p}10", hidden.at[p], held.at[p, 1, 0], behind)
+        send(f"{p}01", hidden.at[p], held.at[p, 0, 1], across)
+    for p in range(2):
+        wide = hidden[p].astype(jnp.float32)
+        squares = jnp.sum(wide * wide, axis=-1, keepdims=True)
+        stat[0, 0, pl.ds(p, 1)] = jnp.transpose(jnp.broadcast_to(squares, (128, 128)))[0:1]
+    for dy, dz in spots[1:]:
+        send(f"t{dy}{dz}", stat.at[0, 0], stat.at[(4 - dy) % 4, dz], at(dy, dz))
+
+    def forward(p, dz):
+        arrived(f"{p}3{dz}")
+        send(f"{p}2{dz}a", held.at[p, 3, dz, pl.ds(0, 64)], held.at[p, 2, dz, pl.ds(0, 64)], ahead)
+        arrived(f"{p}1{dz}")
+        send(f"{p}2{dz}b", held.at[p, 1, dz, pl.ds(64, 64)], held.at[p, 2, dz, pl.ds(64, 64)], behind)
+
+    scales = {}
+
+    def multiply(p, dy, dz):
+        number = order.index((dy, dz))
+        if p == 0 or (dy, dz) not in multiply.loaded:
+            if (dy, dz) not in multiply.loaded:
+                for part in range(3):
+                    loads[number, part].wait()
+                multiply.loaded.add((dy, dz))
+        block = hidden.at[p] if (dy, dz) == (0, 0) else held.at[p, dy, dz]
+        columns = pl.ds(pl.multiple_of(at(dy, dz)[1] * 1024, 1024), 1024)
+        normed = block[...].astype(jnp.float32) * scales[p] * gain[:, columns].astype(jnp.float32)
+        product = jnp.dot(
+            normed.astype(jnp.bfloat16), weight[number], preferred_element_type=jnp.float32
+        )
+        if (dy, dz) == (0, 0):
+            total[p] = product
+        else:
+            total[p] += product
+
+    multiply.loaded = set()
+    arrived(*[f"t{dy}{dz}" for dy, dz in spots[1:]])
+    for p in range(2):
+        sums = stat[0, 0, pl.ds(p, 1)]
+        for dy, dz in spots[1:]:
+            sums = sums + stat[dy, dz, pl.ds(p, 1)]
+        scale = lax.rsqrt(sums * (1.0 / 8192) + EPSILON)
+        scales[p] = jnp.transpose(jnp.broadcast_to(scale, (128, 128)))[:, 0:1]
+        multiply(p, 0, 0)
+    arrived("001")
+    send("031", held.at[0, 0, 1], held.at[0, 3, 1], ahead)
+    send("011", held.at[0, 0, 1], held.at[0, 1, 1], behind)
+    forward(0, 0)
+    forward(1, 0)
+    send("111", held.at[1, 1, 0], held.at[1, 1, 1], across)
+    send("131", held.at[1, 3, 0], held.at[1, 3, 1], across)
+    for spot in ((1, 0), (3, 0), (0, 1)):
+        for p in range(2):
+            if spot == (0, 1) and p == 1:
+                arrived("101")
+            multiply(p, *spot)
+    forward(0, 1)
+    for p in range(2):
+        for n, low in (("a", 0), ("b", 64)):
+            arrived(f"{p}20{n}")
+            if p == 1:
+                rows = pl.ds(low, 64)
+                send(f"121{n}", held.at[1, 2, 0, rows], held.at[1, 2, 1, rows], across)
+    multiply(1, 2, 0)
+    multiply(0, 2, 0)
+    multiply(0, 1, 1)
+    multiply(0, 3, 1)
+    arrived("111", "131")
+    multiply(1, 1, 1)
+    multiply(1, 3, 1)
+    arrived("021a", "021b")
+    multiply(0, 2, 1)
+
+    def finish(p):
+        cos, sin = cosine[p], sine[p]
+
+        def turned(u):
+            return (u * cos + pltpu.roll(u, 64, 1) * sin).astype(jnp.bfloat16)
+
+        for head in range(4):
+            q = turned(total[p, :, head * 128 : (head + 1) * 128])
+            for tree in range(8):
+                low = (p * 4 + head) * 16
+                query[tree, low : low + 16] = q[tree * 16 : tree * 16 + 16]
+        k = turned(total[p, :, 512:640])
+        v = total[p, :, 640:768].astype(jnp.bfloat16)
+        for tree in range(8):
+            key_new[tree, p * 16 : p * 16 + 16] = k[tree * 16 : tree * 16 + 16]
+            value_new[tree, p * 16 : p * 16 + 16] = v[tree * 16 : tree * 16 + 16]
+
+    finish(0)
+    arrived("121a", "121b")
+    multiply(1, 2, 1)
+    finish(1)
+    for copy in made.values():
+        copy.wait_send()
+
+
+def project_call(hidden, gain, cosine, sine, w_query, key_weight, value_weight):
+    bf, f32 = jnp.bfloat16, jnp.float32
+    vm = pl.BlockSpec(memory_space=pltpu.VMEM)
+    anywhere = pl.BlockSpec(memory_space=pl.ANY)
+    return pl.pallas_call(
+        project_kernel,
+        out_shape=(
+            jax.ShapeDtypeStruct((8, 128, 128), bf),
+            jax.ShapeDtypeStruct((8, 32, 128), bf),
+            jax.ShapeDtypeStruct((8, 32, 128), bf),
+        ),
+        in_specs=[vm] * 4 + [anywhere] * 3,
+        out_specs=(vm, vm, vm),
+        scratch_shapes=[
+            pltpu.VMEM((2, 4, 2, 128, 1024), bf),
+            pltpu.VMEM((4, 2, 8, 128), f32),
+            pltpu.VMEM((8, 1024, 768), bf),
+            pltpu.VMEM((2, 128, 768), f32),
+            pltpu.SemaphoreType.DMA((40,)),
+            pltpu.SemaphoreType.DMA((40,)),
+            pltpu.SemaphoreType.DMA((24,)),
+        ],
+        compiler_params=pltpu.CompilerParams(
+            collective_id=1, has_side_effects=True, vmem_limit_bytes=50 * 2**20
+        ),
+        cost_estimate=pl.CostEstimate(flops=4 * 10**9, bytes_accessed=16 * 2**20, transcendentals=0),
+    )(hidden, gain, cosine, sine, w_query, key_weight, value_weight)
+
+
+def rope_tables(row_length):
+    spots = row_length[None, :] + jnp.arange(2, dtype=jnp.int32)[:, None]
+    ladder = jnp.arange(64, dtype=jnp.float32) * (2.0 / 128)
+    frequency = jnp.power(jnp.float32(ROPE_BASE), -ladder)
+    angles = spots.astype(jnp.float32)[..., None] * frequency
+    cosine, sine = jnp.cos(angles), jnp.sin(angles)
+    return jnp.concatenate([cosine, cosine], axis=-1), jnp.concatenate([-sine, sine], axis=-1)
+
+
+def attention_kernel(
+    pages, q_own, key_new, value_new, lim, keys, values,
+    out,
+    q_all, part, part_stat, got, got_stat, relay, relay_stat, rowed, rowed_stat, fresh, fresh_stat,
+    lhs, send_sem, recv_sem,
+):
+    x, zl, core, h = place()
+
+    def at(dx, dz):
+        return (lax.rem(x + dx, 4) * 4 + (zl if dz == 0 else 1 - zl) * 2 + core, h)
+
+    ahead, behind, across = at(1, 0), at(3, 0), at(0, 1)
+    barrier = pltpu.get_barrier_semaphore()
+    for device in (ahead, behind, across):
+        pl.semaphore_signal(barrier, inc=1, device_id=device, device_id_type=MESH)
+    pl.semaphore_wait(barrier, 3)
+
+    made, send, arrived = sender(send_sem, recv_sem)
     lhs[128:144, :] = jnp.ones((16, 1024), jnp.bfloat16)
     token = lax.broadcasted_iota(jnp.int32, (1024, 128), 0) % 64
     low_lanes = lax.broadcasted_iota(jnp.int32, (128, 128), 1) < 64
@@ -273,6 +436,112 @@
     return numbers.reshape(-1), lim
 
 
+def out_kernel(att, w_out, out, sent, got_y, got_z, send_sem, recv_sem):
+    c, y, zh = column_place()
+
+    def at(dy, dz):
+        return (c, lax.rem(y + dy, 4) * 2 + (zh if dz == 0 else 1 - zh))
+
+    ahead, behind, across = at(1, 0), at(3, 0), at(0, 1)
+    barrier = pltpu.get_barrier_semaphore()
+    for device in (ahead, behind, across):
+        pl.semaphore_signal(barrier, inc=1, device_id=device, device_id_type=MESH)
+    pl.semaphore_wait(barrier, 3)
+    made, send, arrived = sender(send_sem, recv_sem)
+
+    def product(dy, dz, p, low, rows):
+        features = pl.ds(pl.multiple_of(at(dy, dz)[1] * 1024, 1024), 1024)
+        return jnp.dot(
+            att[pl.ds(p * 128 + low, rows)], w_out[:, features], preferred_element_type=jnp.float32
+        )
+
+    def ring(p, dz, name, extra):
+        buf, box = sent.at[p, dz], got_y.at[p, dz]
+
+        def term(dy, low, rows):
+            r = product(dy, dz, p, low, rows)
+            return r if extra is None else r + extra[dy, pl.ds(low, rows)].astype(jnp.float32)
+
+        def far():
+            if extra is not None:
+                arrived(f"z{p}2")
+            for low, to, n in ((0, ahead, "a"), (64, behind, "b")):
+                buf[2, pl.ds(low, 64)] = term(2, low, 64).astype(jnp.bfloat16)
+                send(name + "f" + n, buf.at[2, pl.ds(low, 64)], box.at[2, pl.ds(low, 64)], to)
+
+        def near():
+            if extra is not None:
+                arrived(f"z{p}1", f"z{p}3")
+            for dy, low, to, n in ((1, 64, ahead, "a"), (3, 0, behind, "b")):
+                buf[dy, pl.ds(low, 64)] = term(dy, low, 64).astype(jnp.bfloat16)
+                send(name + "n" + n, buf.at[dy, pl.ds(low, 64)], box.at[4 - dy, pl.ds(low, 64)], to)
+
+        def join():
+            for dy, low, to, n in ((1, 0, ahead, "a"), (3, 64, behind, "b")):
+                arrived(name + "f" + n)
+                summed = term(dy, low, 64) + box[2, pl.ds(low, 64)].astype(jnp.float32)
+                buf[dy, pl.ds(low, 64)] = summed.astype(jnp.bfloat16)
+                send(name + "j" + n, buf.at[dy, pl.ds(low, 64)], box.at[4 - dy, pl.ds(low, 64)], to)
+
+        def end():
+            if extra is not None:
+                arrived(f"z{p}0")
+            r = term(0, 0, 128)
+            arrived(*[name + s + n for s in "nj" for n in "ab"])
+            return r + box[1].astype(jnp.float32) + box[3].astype(jnp.float32)
+
+        return far, near, join, end
+
+    first_other = ring(0, 1, "p", None)
+    first_own = ring(0, 0, "q", None)
+    second = ring(1, 0, "r", got_z.at[1])
+    first_other[0]()
+    for dy in (2,):
+        sent[1, 1, dy] = product(dy, 1, 1, 0, 128).astype(jnp.bfloat16)
+        send(f"z1{dy}", sent.at[1, 1, dy], got_z.at[1, dy], across)
+    first_own[0]()
+    for dy in (1, 3, 0):
+        sent[1, 1, dy] = product(dy, 1, 1, 0, 128).astype(jnp.bfloat16)
+        send(f"z1{dy}", sent.at[1, 1, dy], got_z.at[1, dy], across)
+    first_other[1]()
+    first_own[1]()
+    first_other[2]()
+    first_own[2]()
+    second[0]()
+    sent[0, 1, 0] = first_other[3]().astype(jnp.bfloat16)
+    send("z0", sent.at[0, 1, 0], got_z.at[0, 0], across)
+    second[1]()
+    second[2]()
+    half = first_own[3]()
+    arrived("z0")
+    out[0] = (half + got_z[0, 0].astype(jnp.float32)).astype(jnp.bfloat16)
+    out[1] = second[3]().astype(jnp.bfloat16)
+    for copy in made.values():
+        copy.wait_send()
+
+
+def out_call(att, w_out):
+    bf = jnp.bfloat16
+    vm = pl.BlockSpec(memory_space=pltpu.VMEM)
+    return pl.pallas_call(
+        out_kernel,
+        out_shape=jax.ShapeDtypeStruct((2, 128, 1024), bf),
+        in_specs=[vm, vm],
+        out_specs=vm,
+        scratch_shapes=[
+            pltpu.VMEM((2, 2, 4, 128, 1024), bf),
+            pltpu.VMEM((2, 2, 4, 128, 1024), bf),
+            pltpu.VMEM((2, 4, 128, 1024), bf),
+            pltpu.SemaphoreType.DMA((32,)),
+            pltpu.SemaphoreType.DMA((32,)),
+        ],
+        compiler_params=pltpu.CompilerParams(
+            collective_id=3, has_side_effects=True, vmem_limit_bytes=50 * 2**20
+        ),
+        cost_estimate=pl.CostEstimate(flops=2 * 10**9, bytes_accessed=10 * 2**20, transcendentals=0),
+    )(att, w_out)
+
+
 def body(
     hidden,
     norm_gain,
@@ -287,62 +556,19 @@
     row_depth,
     row_length,
 ):
-    positions_n = hidden.shape[0]
-    local_rows = hidden.shape[1]
-    page_size = key_cache.shape[1]
-    kv_local = key_cache.shape[2]
-    head_dim = key_cache.shape[3]
-    query_local = w_query.shape[1] // head_dim
-    full_rows = lax.all_gather(hidden, "head", axis=2, tiled=True)
-    widened = full_rows.astype(jnp.float32)
-    mean_square = jnp.mean(widened * widened, axis=-1, keepdims=True)
-    normalized_input = (
-        widened * lax.rsqrt(mean_square + EPSILON) * norm_gain.astype(jnp.float32)
-    ).astype(jnp.bfloat16)
-    position_list = row_length[None, :] + jnp.arange(positions_n, dtype=jnp.int32)[:, None]
-    query = apply_rotary(
-        jnp.dot(normalized_input, w_query, preferred_element_type=jnp.float32).reshape(
-            positions_n, local_rows, query_local, head_dim
-        ),
-        position_list[:, :, None],
-    ).astype(jnp.bfloat16)
-    fresh_key = apply_rotary(
-        jnp.dot(normalized_input, key_weight, preferred_element_type=jnp.float32).reshape(
-            positions_n, local_rows, kv_local, head_dim
-        ),
-        position_list[:, :, None],
-    ).astype(jnp.bfloat16)
-    fresh_value = (
-        jnp.dot(normalized_input, value_weight, preferred_element_type=jnp.float32)
-        .astype(jnp.bfloat16)
-        .reshape(positions_n, local_rows, kv_local, head_dim)
-    )
-    trees = local_rows // 16
-    own = query.reshape(positions_n, trees, 16, query_local, head_dim).transpose(1, 0, 3, 2, 4)
-    own = own.reshape(trees, 128, head_dim)
-    new_k = fresh_key.reshape(positions_n, trees, 16, head_dim).transpose(1, 0, 2, 3).reshape(trees, 32, head_dim)
-    new_v = fresh_value.reshape(positions_n, trees, 16, head_dim).transpose(1, 0, 2, 3).reshape(trees, 32, head_dim)
-    keys = key_cache.reshape(128, page_size, head_dim)
-    values = jnp.transpose(value_cache.reshape(128, page_size, head_dim), (0, 2, 1))
+    keys = key_cache.reshape(128, 64, 128)
+    values = jnp.transpose(value_cache.reshape(128, 64, 128), (0, 2, 1))
     keys = jnp.concatenate([keys, sibling(keys)], axis=0)
     values = jnp.concatenate([values, sibling(values)], axis=0)
     values = jnp.concatenate([values, values], axis=2)
     numbers, lim = tables(tree_pages, page_fill, row_depth)
-    attention = attention_call(numbers, own, new_k, new_v, lim, keys, values)
-    attention = attention.reshape(trees, positions_n, query_local, 16, head_dim).transpose(1, 0, 3, 2, 4)
-    flat_attention = attention.reshape(positions_n * local_rows, query_local * head_dim)
-    out_rows = w_out.shape[1] // lax.axis_size("head")
-    reduced = lax.psum_scatter(
-        lax.dot_general(
-            w_out, flat_attention, (((0,), (1,)), ((), ())), preferred_element_type=jnp.float32
-        ),
-        "head",
-        scatter_dimension=0,
-        tiled=True,
+    cosine, sine = rope_tables(row_length)
+    query, key_new, value_new = project_call(
+        hidden, norm_gain[None, :], cosine, sine, w_query, key_weight, value_weight
     )
-    return (
-        reduced.reshape(out_rows, positions_n, local_rows).transpose(1, 2, 0).astype(jnp.bfloat16)
-    )
+    attention = attention_call(numbers, query, key_new, value_new, lim, keys, values)
+    attention = attention.reshape(8, 2, 4, 16, 128).transpose(1, 0, 3, 2, 4).reshape(256, 512)
+    return out_call(attention, w_out)
 
 
 def solution(mesh):

time: 286 us -> 174 us (0.61)
  waiting for transfers between devices: 158 us -> 0.01 us
  Pallas kernels: 62.3 us -> 139 us
  matrix products: 13.6 us -> 0 us
  between operations: 13.7 us -> 0.17 us
  other arithmetic: 21.6 us -> 18.6 us
    reduce_scatter x1 -> x0, waiting for transfers between devices: 111 us -> none  [body(): lax.psum_scatter(lax.dot_general(w_out, flat_attention, (((0,), (1,)), ((...]
    pallas_call x0 -> x2, Pallas kernels: none -> 77.2 us  [the longest x1 45 us: project_call(): pl.pallas_call(project_kernel, out_shape=(jax.ShapeDtypeStruct((8, 128, 1...]
    all_gather x1 -> x0, waiting for transfers between devices: 46.3 us -> none  [body(): full_rows = lax.all_gather(hidden, 'head', axis=2, tiled=True)]
    dot_general x4 -> x0, matrix products: 13.6 us -> none  [the longest x1 5.61 us: body(): lax.dot_general(w_out, flat_attention, (((0,), (1,)), ((), ())), preferre...]
    concatenate x1, other arithmetic: 6.87 us -> 11.5 us  [body(): values = jnp.concatenate([values, values], axis=2)]
    reduce_sum x1 -> x0, other arithmetic: 3.25 us -> none  [body(): mean_square = jnp.mean(widened * widened, axis=-1, keepdims=True)]
    unnamed x22 -> x12, local copies, waits for them, and re-layouts: 6.78 us -> 7.32 us
  transfers between devices with their start and end apart: 5 -> 3, of which waited for: 2 -> 0; matrix products, arithmetic and copies ran while one was open for 10% -> 15% of each run, Pallas kernels for 0% -> 26%
where the time goes in v2:
time: 174 us
  Pallas kernels  139 us (80%)
  other arithmetic  18.6 us (11%)
  local copies, waits for them, and re-layouts  15.3 us (9%)
    pallas_call x1, Pallas kernels, attention_call(): pl.pallas_call(attention_kernel, out_shape=jax.ShapeDtypeStruct((8, 128,...  61.7 us
    pallas_call x1, Pallas kernels, project_call(): pl.pallas_call(project_kernel, out_shape=(jax.ShapeDtypeStruct((8, 128, 1...  45 us
    pallas_call x1, Pallas kernels, out_call(): pl.pallas_call(out_kernel, out_shape=jax.ShapeDtypeStruct((2, 128, 1024),...  32.2 us
    concatenate x1, other arithmetic, body(): values = jnp.concatenate([values, values], axis=2)  11.5 us
    unnamed x12, local copies, waits for them, and re-layouts  7.32 us
    ppermute x1, local copies, waits for them, and re-layouts, sibling(): return lax.ppermute(array, 'cache', [(i, i ^ 1) for i in range(16)])  4.88 us
    concatenate x1, other arithmetic, body(): keys = jnp.concatenate([keys, sibling(keys)], axis=0)  3.92 us
  transfers between devices with their start and end apart: 3, of which 0 were waited for; matrix products, arithmetic and copies ran while one was open for 15% of the time, Pallas kernels for 26%

profile of v2, /device:TPU:0, one launch (start us, length us, event | category | flops | bytes accessed | tf_op | source)
XLA Modules:
  0.0 173.7 jit_solution(4085300959898500795)
XLA Ops:
  0.0 0.5 broadcast.34
  0.5 1.4 reduce.3
  2.0 0.8 copy.23
  2.8 0.8 copy.24
  3.5 0.1 pad_add_fusion.1
  3.7 0.6 collective-permute-start
  4.4 0.7 broadcast_in_dim.27.gain
  5.1 0.7 add_convert_fusion
  5.8 0.5 fusion.2
  6.3 0.1 pad_maximum_fusion.1
  6.5 1.6 copy-done
  8.1 1.0 copy-done.1
  9.1 45.0 %shard_map.118 = (bf16[8,128,128]{2,1,0:T(8,128)(2,1)S(1)}, bf16[8,32,128]{2,1,0:T(8,128)(2,1)S(1)}, bf16[8,32,128]{2,1,0:T(8,128)(2,1)S(1)}) custom-call(bf16[2,128,1024]{2,1,0:T(8,128)(2,1)S(1)} %copy-done.1, bf16[1,8192]{1,0:T(2,128)(2,1)S(1)} %broadcast_in_dim.27.gain, f32[2,128,128]{2,1,0:T(8,128)S(1)} %get-tuple-element.20.cosine, ...), custom_call_target="tpu_custom_call" | custom-call | flops 4000000000 | bytes 16777216 | tf_op jit(solution)/shard_map/pallas_call | solution.py:184
  54.3 3.3 %copy.19 = bf16[128,64,1,128]{1,3,0,2:T(8,128)(2,1)} copy(bf16[128,64,1,128]{3,1,2,0:T(8,128)(2,1)S(1)} %copy-done.2) | data formatting | bytes 4194304 | tf_op args[7]
  57.7 0.1 tile.17
  58.1 0.1 tile.19
  58.3 0.2 fusion
  58.5 4.9 %copy.21 = bf16[128,128,64]{2,1,0:T(8,128)(2,1)} copy(bf16[128,128,64]{1,2,0:T(8,128)(2,1)} %collective-permute-done.2) | data formatting | bytes 4194304 | tf_op jit(solution)/shard_map/ppermute | solution.py:417
  63.4 11.5 %maximum_maximum_fusion.values = bf16[256,128,128]{2,1,0:T(8,128)(2,1)} fusion(bf16[128,128,64]{2,1,0:T(8,128)(2,1)} %copy.21, bf16[128,128,64]{2,1,0:T(8,128)(2,1)} %bitcast.26), kind=kLoop, calls=%fused_computation | loop fusion | flops 33554432 | bytes 12582912 | tf_op jit(solution)/shard_map/concatenate | solution.py:563
  74.9 3.9 %pad_maximum_fusion.keys = bf16[256,64,128]{2,1,0:T(8,128)(2,1)} fusion(bf16[128,64,128]{2,1,0:T(8,128)(2,1)} %collective-permute-done.1, bf16[128,64,128]{2,1,0:T(8,128)(2,1)S(1)} %bitcast.29), kind=kLoop, calls=%fused_computation.1 | loop fusion | flops 2097152 | bytes 8388608 | tf_op jit(solution)/shard_map/concatenate | solution.py:561
  78.9 61.7 %shard_map.119 = bf16[8,128,128]{2,1,0:T(8,128)(2,1)S(1)} custom-call(s32[1024]{0:T(1024)S(1)} %reshape.57.pages, bf16[2,4,128,128]{3,2,1,0:T(8,128)(2,1)S(1)} %bitcast.25, bf16[8,32,128]{2,1,0:T(8,128)(2,1)S(1)} %get-tuple-element.9.key_new, bf16[8,32,128]{2,1,0:T(8,128)(2,1)S(1)} %get-tuple-element.10.value_new, s32[8,8,16,128]{3,2,1,0:T(8,128)S(1)} %pad_add_fusion.lim, ...), custom_call_target="tpu_custom_call" | custom-call | flops 8999999488 | bytes 16777216 | tf_op jit(solution)/shard_map/pallas_call | solution.py:388
  140.6 0.1 copy.22
  140.8 32.2 %shard_map.120 = bf16[2,128,1024]{2,1,0:T(8,128)(2,1)S(1)} custom-call(bf16[256,512]{1,0:T(8,128)(2,1)S(1)} %bitcast.23, bf16[512,8192]{1,0:T(8,128)(2,1)} %w_out.1), custom_call_target="tpu_custom_call" | custom-call | flops 2000000000 | bytes 10485760 | tf_op jit(solution)/shard_map/pallas_call | solution.py:526
  172.9 0.8 copy.30
  (24 shorter events, 0.8 us)
Async XLA Ops:
  0.0 58.5 %collective-permute-start.2 = (bf16[128,128,64]{1,2,0:T(8,128)(2,1)}, bf16[128,128,64]{1,2,0:T(8,128)(2,1)}, u32[]{:S(2)}, u32[]{:S(2)}) collective-permute-start(bf16[128,128,64]{1,2,0:T(8,128)(2,1)} %bitcast.27), channel_id=1, source_target_pairs={{0,8},{8,0},{16,24},{24,16},{32,40},{40,32},{48,56},{56,48},{64,72... | collective-permute-start | bytes 6291464 | tf_op jit(solution)/shard_map/ppermute | solution.py:417
  3.7 54.1 %collective-permute-start = (s32[8,8,32]{2,1,0:T(8,128)S(1)}, s32[8,8,32]{2,1,0:T(8,128)S(1)}, u32[]{:S(2)}, u32[]{:S(2)}) collective-permute-start(s32[8,8,32]{2,1,0:T(8,128)S(1)} %get-tuple-element.12), channel_id=1, source_target_pairs={{0,8},{8,0},{16,24},{24,16},{32,40},{40,32},{48,56},{56,48},{64,72... | collective-permute-start | bytes 24584 | tf_op jit(solution)/shard_map/ppermute | solution.py:417
  4.3 70.7 %collective-permute-start.1 = (bf16[128,64,128]{2,1,0:T(8,128)(2,1)}, bf16[128,64,128]{2,1,0:T(8,128)(2,1)}, u32[]{:S(2)}, u32[]{:S(2)}) collective-permute-start(bf16[128,64,128]{2,1,0:T(8,128)(2,1)} %bitcast.28), channel_id=1, source_target_pairs={{0,8},{8,0},{16,24},{24,16},{32,40},{40,32},{48,56},{56,48},{64,72... | collective-permute-start | bytes 6291464 | tf_op jit(solution)/shard_map/ppermute | solution.py:417
  6.5 1.6 copy-start
  8.0 1.0 copy-start.1
  9.1 45.2 %copy-start.2 = (bf16[128,64,1,128]{3,1,2,0:T(8,128)(2,1)S(1)}, bf16[128,64,1,128]{3,1,2,0:T(8,128)(2,1)}, u32[]{:S(2)}) copy-start(bf16[128,64,1,128]{3,1,2,0:T(8,128)(2,1)} %param.19) | copy-start | bytes 6291460
  63.4 11.5 %copy-start.3 = (bf16[128,64,1,128]{3,1,2,0:T(8,128)(2,1)S(1)}, bf16[128,64,1,128]{3,1,2,0:T(8,128)(2,1)}, u32[]{:S(2)}) copy-start(bf16[128,64,1,128]{3,1,2,0:T(8,128)(2,1)} %param.18) | copy-start | bytes 6291460

commit v3 on v0

v3 whole, which is shorter than its diff:
```python
import math

import jax
import jax.numpy as jnp
from jax import lax
from jax.experimental import pallas as pl
from jax.experimental.pallas import tpu as pltpu
from jax.sharding import PartitionSpec as P

MESH = pl.DeviceIdType.MESH
ROPE_BASE = 500000.0
EPSILON = 1e-05
LOW_SCORE = -1e30
LOW_MAX = -1e29
EXP_SCALE = math.log2(math.e) / math.sqrt(128.0)
BF, F32 = jnp.bfloat16, jnp.float32
SPOTS = [(dy, dz) for dy in range(4) for dz in range(2)]
ORDER = [(0, 0), (1, 0), (3, 0), (0, 1), (2, 0), (1, 1), (3, 1), (2, 1)]


def kernel(
    hidden, gain, cosine, sine, pages_in, fill, depth, w_query, key_weight, value_weight, w_out_hbm, key_hbm, value_hbm,
    out,
    held, sums, scale, weight, total, w_out, keys, values, filled, bias, bias_away, pages_away, pages,
    q_all, key_new, value_new, part, part_stat, got, got_stat, relay, relay_stat, rowed, rowed_stat, fresh, fresh_stat,
    vals, att, sent, got_y, got_z,
    send_sem, recv_sem, load_sem,
):
    c, h = lax.axis_index("cache"), lax.axis_index("head")
    x, zl, core = c // 4, lax.rem(c // 2, 2), lax.rem(c, 2)
    y, zh = h // 2, lax.rem(h, 2)

    def in_head(dy, dz):
        return lax.rem(y + dy, 4) * 2 + (zh if dz == 0 else 1 - zh)

    def in_cache(dx, dz):
        return lax.rem(x + dx, 4) * 4 + (zl if dz == 0 else 1 - zl) * 2 + core

    y_up, y_down, z_far = (c, in_head(1, 0)), (c, in_head(3, 0)), (c, in_head(0, 1))
    x_up, x_down, z_near = (in_cache(1, 0), h), (in_cache(3, 0), h), (in_cache(0, 1), h)
    twin = (c + 1 - 2 * core, h)

    loads = {}

    def load(name, src, dst):
        loads[name] = pltpu.make_async_copy(src, dst, load_sem.at[len(loads)])
        loads[name].start()

    load("pages", pages_in.at[core], pages.at[0])
    for number, spot in enumerate(ORDER):
        rows = pl.ds(pl.multiple_of(in_head(*spot) * 1024, 1024), 1024)
        load(("q", number), w_query.at[rows], weight.at[number, :, pl.ds(0, 512)])
        load(("k", number), key_weight.at[rows], weight.at[number, :, pl.ds(512, 128)])
        load(("v", number), value_weight.at[rows], weight.at[number, :, pl.ds(640, 128)])
    load("keys", key_hbm, keys.at[pl.ds(0, 128)])
    load("values", value_hbm, values.at[pl.ds(0, 128)])
    load("out", w_out_hbm, w_out)

    barrier = pltpu.get_barrier_semaphore()
    others = [(c, in_head(*spot)) for spot in SPOTS[1:]] + [x_up, x_down, z_near, twin]
    for device in others:
        pl.semaphore_signal(barrier, inc=1, device_id=device, device_id_type=MESH)
    pl.semaphore_wait(barrier, len(others))

    made = {}

    def send(name, src, dst, device):
        number = len(made)
        made[name] = pltpu.make_async_remote_copy(
            src_ref=src, dst_ref=dst, send_sem=send_sem.at[number], recv_sem=recv_sem.at[number],
            device_id=device, device_id_type=MESH,
        )
        made[name].start()

    def arrived(*names):
        for name in names:
            made[name].wait_recv()


    def gather_start(half):
        rows = pl.ds(half * 64, 64)
        for p in range(2):
            for name, to, dy, dz in (("30", y_up, 3, 0), ("10", y_down, 1, 0), ("01", z_far, 0, 1)):
                send(f"a{half}{p}{name}", hidden.at[p, rows], held.at[half, dy, dz, p], to)

    low_rows, high_rows = pl.ds(0, 32), pl.ds(32, 32)

    def gather_forward(half, p, dz):
        a = f"a{half}{p}"
        arrived(f"{a}3{dz}")
        send(f"{a}2{dz}u", held.at[half, 3, dz, p, low_rows], held.at[half, 2, dz, p, low_rows], y_up)
        arrived(f"{a}1{dz}")
        send(f"{a}2{dz}d", held.at[half, 1, dz, p, high_rows], held.at[half, 2, dz, p, high_rows], y_down)

    def gather_second(half):
        arrived(f"a{half}001")
        send(f"a{half}031", held.at[half, 0, 1, 0], held.at[half, 3, 1, 0], y_up)
        send(f"a{half}011", held.at[half, 0, 1, 0], held.at[half, 1, 1, 0], y_down)
        gather_forward(half, 0, 0)
        gather_forward(half, 1, 0)
        send(f"a{half}111", held.at[half, 1, 0, 1], held.at[half, 1, 1, 1], z_far)
        send(f"a{half}131", held.at[half, 3, 0, 1], held.at[half, 3, 1, 1], z_far)

    def gather_third(half):
        gather_forward(half, 0, 1)
        for n, rows in (("u", low_rows), ("d", high_rows)):
            arrived(f"a{half}120{n}")
            send(f"a{half}121{n}", held.at[half, 2, 0, 1, rows], held.at[half, 2, 1, 1, rows], z_far)

    ready = set()

    def multiply(half, dy, dz):
        number = ORDER.index((dy, dz))
        if number not in ready:
            for array in "qkv":
                loads[array, number].wait()
            ready.add(number)
        if (dy, dz) == (0, 0):
            rows = pl.ds(half * 64, 64)
            block = jnp.concatenate([hidden[0, rows], hidden[1, rows]], axis=0)
        else:
            block = held[half, dy, dz].reshape(128, 1024)
        columns = pl.ds(pl.multiple_of(in_head(dy, dz) * 1024, 1024), 1024)
        normed = block.astype(F32) * scale[half][:, 0:1] * gain[:, columns].astype(F32)
        product = jnp.dot(normed.astype(BF), weight[number], preferred_element_type=F32)
        if (dy, dz) == (0, 0):
            total[half] = product
        else:
            total[half] += product

    def multiply_near(half):
        arrived(f"a{half}101")
        for spot in ((1, 0), (3, 0), (0, 1)):
            multiply(half, *spot)

    def multiply_mid(half):
        arrived(f"a{half}020u", f"a{half}020d")
        multiply(half, 2, 0)
        arrived(f"a{half}111", f"a{half}131")
        multiply(half, 1, 1)
        multiply(half, 3, 1)

    def multiply_far(half):
        arrived(*[f"a{half}{p}21{n}" for p in range(2) for n in "ud"])
        multiply(half, 2, 1)

    def project_end(half):
        rows = pl.ds(half * 64, 64)
        cos = jnp.concatenate([cosine[0, rows], cosine[1, rows]], axis=0)
        sin = jnp.concatenate([sine[0, rows], sine[1, rows]], axis=0)

        def turned(u):
            return (u * cos + pltpu.roll(u, 64, 1) * sin).astype(BF)

        k = turned(total[half, :, 512:640])
        v = total[half, :, 640:768].astype(BF)
        for head in range(4):
            q = turned(total[half, :, head * 128 : (head + 1) * 128])
            for p in range(2):
                for u in range(4):
                    low = (p * 4 + head) * 16
                    q_all[0, 0, half, u, low : low + 16] = q[p * 64 + u * 16 : p * 64 + u * 16 + 16]
        for p in range(2):
            for u in range(4):
                low, there = p * 64 + u * 16, u * 32 + p * 16
                key_new[half, there : there + 16] = k[low : low + 16]
                value_new[half, there : there + 16, 0:128] = v[low : low + 16]


    def query_start(half):
        q = f"q{half}"
        send(q + "30", q_all.at[0, 0, half], q_all.at[3, 0, half], x_up)
        send(q + "10", q_all.at[0, 0, half], q_all.at[1, 0, half], x_down)
        send(q + "01", q_all.at[0, 0, half], q_all.at[0, 1, half], z_near)

    def query_forward(half, dz):
        q = f"q{half}"
        lows, highs = pl.ds(0, 2), pl.ds(2, 2)
        arrived(f"{q}3{dz}")
        send(f"{q}2{dz}u", q_all.at[3, dz, half, lows], q_all.at[2, dz, half, lows], x_up)
        arrived(f"{q}1{dz}")
        send(f"{q}2{dz}d", q_all.at[1, dz, half, highs], q_all.at[2, dz, half, highs], x_down)

    def query_second(half):
        q = f"q{half}"
        arrived(q + "01")
        send(q + "31", q_all.at[0, 1, half], q_all.at[3, 1, half], x_up)
        send(q + "11", q_all.at[0, 1, half], q_all.at[1, 1, half], x_down)
        query_forward(half, 0)


    lane = lax.broadcasted_iota(jnp.int32, (128, 128), 1)
    row = lax.broadcasted_iota(jnp.int32, (128, 128), 0)

    def fresh_tokens(half):
        stats = jnp.zeros((128, 128), F32)
        for u in range(4):
            seen = (lane // 32 == u) & (lane % 16 == row % 16) & ((lane % 32) // 16 <= row // 64)
            s = lax.dot_general(
                q_all[0, 0, half, u], key_new[half], (((1,), (1,)), ((), ())), preferred_element_type=F32
            )
            s = jnp.where(seen, s, LOW_SCORE)
            m = jnp.max(s, axis=1, keepdims=True)
            p = jnp.exp2((s - m) * EXP_SCALE).astype(BF)
            o = jnp.dot(p, value_new[half], preferred_element_type=F32)
            fresh[half, u] = o[:, 0:128].astype(BF)
            stats = jnp.where(lane == u, m, stats)
            stats = jnp.where(lane == u + 4, o[:, 128:256], stats)
        fresh_stat[half] = jnp.transpose(stats)[0:8]

    def block(half, dx, dz):
        owner = lax.rem(x + dx, 4) * 2 + (zl if dz == 0 else 1 - zl)
        stats = jnp.zeros((128, 128), F32)
        for u in range(4):
            tree = owner * 8 + half * 4 + u
            base = tree * 8
            numbers = []
            for b in range(2):
                numbers += [pages[b, base // 128, lax.rem(base, 128) + i] + b * 128 for i in range(8)]
            k = jnp.concatenate([keys[n] for n in numbers], axis=0)
            s = lax.dot_general(
                q_all[dx, dz, half, u], k, (((1,), (1,)), ((), ())), preferred_element_type=F32
            )
            hide = jnp.concatenate([bias[0, tree], bias[1, tree]], axis=1).astype(F32)
            s = jnp.concatenate([s[i * 16 : (i + 1) * 16] + hide for i in range(8)], axis=0)
            m = jnp.maximum(jnp.max(s, axis=1, keepdims=True), LOW_MAX)
            p = jnp.exp2((s - m) * EXP_SCALE).astype(BF)
            for i in range(16):
                vals[u, i * 64 : (i + 1) * 64, 0:128] = values[numbers[i]]
            o = jnp.dot(p, vals[u], preferred_element_type=F32)
            part[dx, dz, half, u] = o[:, 0:128].astype(BF)
            stats = jnp.where(lane == u, m, stats)
            stats = jnp.where(lane == u + 4, o[:, 128:256], stats)
        part_stat[dx, dz, half] = jnp.transpose(stats)[0:8]
        n = f"{half}{dx}{dz}"
        if dx in (1, 3):
            to, slot = (x_up, 0) if dx == 1 else (x_down, 1)
            send("o" + n, part.at[dx, dz, half], got.at[slot, dz, half], to)
            send("s" + n, part_stat.at[dx, dz, half], got_stat.at[slot, dz, half], to)
        if dx == 2:
            to = x_up if dz == 0 else x_down
            send("o" + n, part.at[dx, dz, half], relay.at[dz, half], to)
            send("s" + n, part_stat.at[dx, dz, half], relay_stat.at[dz, half], to)

    def pass_on(half, dz):
        n = f"{half}2{dz}"
        to = x_up if dz == 0 else x_down
        arrived("o" + n, "s" + n)
        send("ro" + n, relay.at[dz, half], got.at[2, dz, half], to)
        send("rs" + n, relay_stat.at[dz, half], got_stat.at[2, dz, half], to)

    def weigh(stats):
        tops = [s[0:4] for s in stats]
        top = tops[0]
        for other in tops[1:]:
            top = jnp.maximum(top, other)
        weights = [jnp.exp2((m - top) * EXP_SCALE) for m in tops]
        summed = jnp.zeros((4, 128), F32)
        for w, s in zip(weights, stats):
            summed = summed + w * s[4:8]
        return top, weights, summed

    def columns_of(weights):
        stacked = jnp.concatenate(weights + [jnp.zeros((128 - 4 * len(weights), 128), F32)], axis=0)
        return jnp.transpose(stacked)

    def received(half, dz):
        n = f"{half}{{}}{dz}"
        for a in "os":
            arrived(a + n.format(1), a + n.format(3), "r" + a + n.format(2))

    def plane_merge(half):
        received(half, 1)
        outs = [part.at[0, 1, half]] + [got.at[i, 1, half] for i in range(3)]
        top, weights, summed = weigh([part_stat[0, 1, half]] + [got_stat[i, 1, half] for i in range(3)])
        columns = columns_of(weights)
        for u in range(4):
            o = jnp.zeros((128, 128), F32)
            for i, ref in enumerate(outs):
                o = o + columns[:, i * 4 + u : i * 4 + u + 1] * ref[u].astype(F32)
            rowed[0, half, u] = o.astype(BF)
        rowed_stat[0, half] = jnp.concatenate([top, summed], axis=0)
        send(f"zo{half}", rowed.at[0, half], rowed.at[1, half], z_near)
        send(f"zs{half}", rowed_stat.at[0, half], rowed_stat.at[1, half], z_near)

    def last_merge(half):
        received(half, 0)
        arrived(f"zo{half}", f"zs{half}")
        outs = [part.at[0, 0, half]] + [got.at[i, 0, half] for i in range(3)] + [rowed.at[1, half], fresh.at[half]]
        stats = [part_stat[0, 0, half]] + [got_stat[i, 0, half] for i in range(3)]
        stats += [rowed_stat[1, half], fresh_stat[half]]
        top, weights, summed = weigh(stats)
        columns = columns_of([w / summed for w in weights])
        for u in range(4):
            o = jnp.zeros((128, 128), F32)
            for i, ref in enumerate(outs):
                o = o + columns[:, i * 4 + u : i * 4 + u + 1] * ref[u].astype(F32)
            o = o.astype(BF)
            for p in range(2):
                for head in range(4):
                    low = (p * 4 + head) * 16
                    att[half, p * 64 + u * 16 : p * 64 + u * 16 + 16, head * 128 : (head + 1) * 128] = o[low : low + 16]


    rings = {"p": (0, 0, 1), "q": (1, 0, 0), "r": (2, 1, 0)}

    def product(half, dy, dz):
        features = pl.ds(pl.multiple_of(in_head(dy, dz) * 1024, 1024), 1024)
        r = jnp.dot(att[half], w_out[:, features], preferred_element_type=F32).astype(BF)
        sent[half, dz, dy] = r.reshape(2, 64, 1024)

    def over_z(half, dy):
        send(f"z{half}{dy}", sent.at[half, 1, dy, 1], got_z.at[half, dy], z_far)

    def add_z(half, dy):
        arrived(f"z{half}{dy}")
        sent[half, 0, dy, 1] = (sent[half, 0, dy, 1].astype(F32) + got_z[half, dy].astype(F32)).astype(BF)

    def ring_far(half, name):
        ring, p, dz = rings[name]
        for rows, to, n in ((low_rows, y_up, "u"), (high_rows, y_down, "d")):
            send(f"{name}f{half}{n}", sent.at[half, dz, 2, p, rows], got_y.at[half, ring, 0, rows], to)

    def ring_near(half, name):
        ring, p, dz = rings[name]
        for dy, rows, to, n, slot in ((1, high_rows, y_up, "u", 2), (3, low_rows, y_down, "d", 1)):
            send(f"{name}n{half}{n}", sent.at[half, dz, dy, p, rows], got_y.at[half, ring, slot, rows], to)

    def ring_join(half, name):
        ring, p, dz = rings[name]
        for dy, rows, to, n, slot in ((1, low_rows, y_up, "u", 2), (3, high_rows, y_down, "d", 1)):
            arrived(f"{name}f{half}{n}")
            summed = sent[half, dz, dy, p, rows].astype(F32) + got_y[half, ring, 0, rows].astype(F32)
            sent[half, dz, dy, p, rows] = summed.astype(BF)
            send(f"{name}j{half}{n}", sent.at[half, dz, dy, p, rows], got_y.at[half, ring, slot, rows], to)

    def ring_end(half, name):
        ring, p, dz = rings[name]
        arrived(*[f"{name}{s}{half}{n}" for s in "nj" for n in "ud"])
        r = sent[half, dz, 0, p].astype(F32)
        return r + got_y[half, ring, 1].astype(F32) + got_y[half, ring, 2].astype(F32)

    def out_start(half):
        product(half, 2, 1)
        ring_far(half, "p")
        over_z(half, 2)
        product(half, 2, 0)
        ring_far(half, "q")
        product(half, 1, 1)
        over_z(half, 1)
        product(half, 3, 1)
        over_z(half, 3)
        ring_near(half, "p")
        product(half, 0, 1)
        over_z(half, 0)
        product(half, 1, 0)
        product(half, 3, 0)
        ring_near(half, "q")
        product(half, 0, 0)

    def out_join(half):
        ring_join(half, "p")
        ring_join(half, "q")

    def out_second(half):
        add_z(half, 2)
        ring_far(half, "r")
        add_z(half, 1)
        add_z(half, 3)
        ring_near(half, "r")

    def out_cross(half):
        sent[half, 1, 0, 0] = ring_end(half, "p").astype(BF)
        send(f"y{half}", sent.at[half, 1, 0, 0], got_z.at[half, 4], z_far)

    def out_third(half):
        ring_join(half, "r")
        add_z(half, 0)

    def out_end(half):
        rows = pl.ds(half * 64, 64)
        first = ring_end(half, "q")
        arrived(f"y{half}")
        out[0, rows] = (first + got_z[half, 4].astype(F32)).astype(BF)
        out[1, rows] = ring_end(half, "r").astype(BF)


    def exchange_start():
        send("pages", pages_in.at[1 - core], pages_away, twin)
        send("keys", key_hbm, keys.at[pl.ds(128, 128)], twin)
        send("values", value_hbm, values.at[pl.ds(128, 128)], twin)

    def squares_start():
        for p in range(2):
            wide = hidden[p].astype(F32)
            squares = jnp.sum(wide * wide, axis=-1, keepdims=True)
            sums[0, 0, pl.ds(p, 1)] = jnp.transpose(jnp.broadcast_to(squares, (128, 128)))[0:1]
        for dy, dz in SPOTS[1:]:
            send(f"t{dy}{dz}", sums.at[0, 0], sums.at[(4 - dy) % 4, dz], (c, in_head(dy, dz)))

    def squares_end():
        arrived(*[f"t{dy}{dz}" for dy, dz in SPOTS[1:]])
        for p in range(2):
            s = sums[0, 0, pl.ds(p, 1)]
            for dy, dz in SPOTS[1:]:
                s = s + sums[dy, dz, pl.ds(p, 1)]
            s = jnp.transpose(jnp.broadcast_to(lax.rsqrt(s * (1.0 / 8192) + EPSILON), (128, 128)))
            for half in range(2):
                scale[half, p * 64 : p * 64 + 64] = s[half * 64 : half * 64 + 64]

    def visibility():
        slot_row = lax.broadcasted_iota(jnp.int32, (128, 512), 0)
        slot_lane = lax.broadcasted_iota(jnp.int32, (128, 512), 1) // 64
        spread = jnp.where(slot_row == slot_lane, 1.0, 0.0).astype(BF)
        filled[...] = jnp.dot(fill[...], spread, preferred_element_type=F32)
        column = lax.broadcasted_iota(jnp.int32, (16, 512), 1)
        slot_of, token_of = (column // 64).astype(F32), (column % 64).astype(F32)

        def group(target, j, e):
            depths = jnp.transpose(jnp.broadcast_to(depth[pl.ds(e, 1)], (128, 128)))
            fills = filled[pl.ds(pl.multiple_of(e * 8, 8), 8)]
            for t in range(8):
                d = jnp.concatenate([depths[t * 16 : t * 16 + 16]] * 4, axis=1)
                visible = (slot_of < d) & (token_of < fills[t : t + 1])
                target[j * 8 + t] = jnp.where(visible, 0.0, LOW_SCORE).astype(BF)

        def away(j, _):
            group(bias_away, j, j * 2 + 1 - core)
            return 0

        def here(j, _):
            group(bias.at[0], j, j * 2 + core)
            return 0

        lax.fori_loop(0, 8, away, 0)
        send("bias", bias_away, bias.at[1], twin)
        lax.fori_loop(0, 8, here, 0)

    def exchange_end():
        arrived("pages")
        load("pages_away", pages_away, pages.at[1])
        for u in range(4):
            vals[u, :, 128:256] = jnp.ones((1024, 128), BF)
        for half in range(2):
            value_new[half, :, 128:256] = jnp.ones((128, 128), BF)
        for name in ("pages", "pages_away", "keys", "values", "out"):
            loads[name].wait()
        arrived("keys", "values", "bias")

    gather_start(0)
    squares_start()
    exchange_start()
    visibility()
    squares_end()
    multiply(0, 0, 0)
    gather_second(0)
    gather_start(1)
    multiply(1, 0, 0)
    multiply_near(0)
    gather_third(0)
    multiply_mid(0)
    gather_second(1)
    exchange_end()
    multiply_far(0)
    project_end(0)
    query_start(0)
    gather_third(1)
    fresh_tokens(0)
    block(0, 0, 0)
    multiply_near(1)
    query_second(0)
    multiply_mid(1)
    block(0, 1, 0)
    block(0, 3, 0)
    multiply_far(1)
    project_end(1)
    query_start(1)
    fresh_tokens(1)
    arrived("q020u", "q020d")
    block(0, 2, 0)
    query_forward(0, 1)
    block(0, 1, 1)
    block(0, 3, 1)
    query_second(1)
    pass_on(0, 0)
    arrived("q021u", "q021d")
    block(0, 2, 1)
    block(0, 0, 1)
    block(1, 0, 0)
    query_forward(1, 1)
    pass_on(0, 1)
    block(1, 1, 0)
    block(1, 3, 0)
    plane_merge(0)
    arrived("q120u", "q120d")
    block(1, 2, 0)
    block(1, 1, 1)
    last_merge(0)
    out_start(0)
    block(1, 3, 1)
    pass_on(1, 0)
    arrived("q121u", "q121d")
    block(1, 2, 1)
    out_join(0)
    block(1, 0, 1)
    out_second(0)
    pass_on(1, 1)
    out_cross(0)
    plane_merge(1)
    out_third(0)
    last_merge(1)
    out_start(1)
    out_end(0)
    out_join(1)
    out_second(1)
    out_cross(1)
    out_third(1)
    out_end(1)
    for copy in made.values():
        copy.wait_send()


def call(*operands):
    vm = pl.BlockSpec(memory_space=pltpu.VMEM)
    anywhere = pl.BlockSpec(memory_space=pl.ANY)
    trees, tile = (4, 128, 128), (8, 128)
    shapes = [
        ((2, 4, 2, 2, 64, 1024), BF), ((4, 2) + tile, F32), ((2, 128, 128), F32), ((8, 1024, 768), BF),
        ((2, 128, 768), F32), ((512, 8192), BF), ((256, 64, 128), BF), ((256, 64, 128), BF), ((128, 512), F32),
        ((2, 64, 16, 512), BF), ((64, 16, 512), BF), (tile, jnp.int32), None,
        ((4, 2, 2) + trees, BF), ((2, 128, 128), BF), ((2, 128, 256), BF),
        ((4, 2, 2) + trees, BF), ((4, 2, 2) + tile, F32), ((3, 2, 2) + trees, BF), ((3, 2, 2) + tile, F32),
        ((2, 2) + trees, BF), ((2, 2) + tile, F32), ((2, 2) + trees, BF), ((2, 2) + tile, F32),
        ((2,) + trees, BF), ((2,) + tile, F32),
        ((4, 1024, 256), BF), ((2, 128, 512), BF), ((2, 2, 4, 2, 64, 1024), BF), ((2, 3, 3, 64, 1024), BF),
        ((2, 5, 64, 1024), BF),
    ]
    scratch = [pltpu.VMEM(*s) if s else pltpu.SMEM((2, 8, 128), jnp.int32) for s in shapes]
    return pl.pallas_call(
        kernel,
        out_shape=jax.ShapeDtypeStruct((2, 128, 1024), BF),
        in_specs=[vm] * 7 + [anywhere] * 6,
        out_specs=vm,
        scratch_shapes=scratch
        + [pltpu.SemaphoreType.DMA((176,)), pltpu.SemaphoreType.DMA((176,)), pltpu.SemaphoreType.DMA((32,))],
        compiler_params=pltpu.CompilerParams(
            collective_id=1, has_side_effects=True, vmem_limit_bytes=61 * 2**20
        ),
        cost_estimate=pl.CostEstimate(flops=15 * 10**9, bytes_accessed=30 * 2**20, transcendentals=10**7),
    )(*operands)


def rope_tables(row_length):
    spots = row_length[None, :] + jnp.arange(2, dtype=jnp.int32)[:, None]
    ladder = jnp.arange(64, dtype=F32) * (2.0 / 128)
    frequency = jnp.power(jnp.float32(ROPE_BASE), -ladder)
    angles = spots.astype(F32)[..., None] * frequency
    cosine, sine = jnp.cos(angles), jnp.sin(angles)
    return jnp.concatenate([cosine, cosine], axis=-1), jnp.concatenate([-sine, sine], axis=-1)


def body(
    hidden,
    norm_gain,
    w_query,
    key_weight,
    value_weight,
    w_out,
    key_cache,
    value_cache,
    tree_pages,
    page_fill,
    row_depth,
    row_length,
):
    cosine, sine = rope_tables(row_length)
    pages = tree_pages.reshape(8, 2, 64).transpose(1, 0, 2).reshape(2, 4, 128)
    pages = jnp.pad(pages, ((0, 0), (0, 4), (0, 0)))
    fill = jnp.pad(page_fill[0].astype(BF), ((0, 0), (0, 120)))
    depth = row_depth.reshape(16, 128).astype(F32)
    return call(
        hidden, norm_gain[None, :], cosine, sine, pages, fill, depth, w_query, key_weight, value_weight, w_out,
        key_cache.reshape(128, 64, 128), value_cache.reshape(128, 64, 128),
    )


def solution(mesh):
    in_specs = (
        P(None, "cache", "head"),
        P(),
        P(None, "head"),
        P(None, "head"),
        P(None, "head"),
        P("head", None),
        P("cache", None, "head", None),
        P("cache", None, "head", None),
        P("cache", None, None),
        P("cache", None, None),
        P("cache", None),
        P("cache"),
    )
    out_specs = P(None, "cache", "head")
    return jax.shard_map(body, mesh=mesh, in_specs=in_specs, out_specs=out_specs, check_vma=False)
```

time: 1040 us -> 125 us (0.12)
  waiting for transfers between devices: 452 us -> 0 us
  local copies, waits for them, and re-layouts: 330 us -> 6.15 us
  other arithmetic: 124 us -> 3.35 us
  Pallas kernels: 0 us -> 116 us
  matrix products: 94.2 us -> 0 us
  starting transfers between devices: 14.7 us -> 0 us
  between operations: 13.9 us -> 0.03 us
    ppermute x124 -> x0, waiting for transfers between devices: 279 us -> none  [passed_along(): lax.ppermute(shard, axis, [(i, (i + by) % length) for i in range(length)])]
    gather x62 -> x0, local copies, waits for them, and re-layouts: 174 us -> none  [the longest x31 101 us: cache_part(): key_cache[page_numbers].reshape(tree_count, key_width, kv_local, head_dim)]
    pallas_call x0 -> x1, Pallas kernels: none -> 116 us  [call(): pl.pallas_call(kernel, out_shape=jax.ShapeDtypeStruct((2, 128, 1024), BF)...]
    reduce_scatter x1 -> x0, waiting for transfers between devices: 110 us -> none  [body(): lax.psum_scatter(lax.dot_general(w_out, flat_attention, (((0,), (1,)), ((...]
    dot_general x70 -> x0, matrix products: 94.2 us -> none  [the longest x32 58.9 us: cache_part(): jnp.einsum('trkxd,tnkd->trkxn', grouped_queries, paged_keys, preferred_el...]
    all_gather x1 -> x0, waiting for transfers between devices: 62.6 us -> none  [body(): full_rows = lax.all_gather(hidden, 'head', axis=2, tiled=True)]
    dynamic_slice x62 -> x0, local copies, waits for them, and re-layouts: 42.8 us -> none  [the longest x31 22 us: cache_part(): lax.dynamic_slice_in_dim(page_fill[0], first_tree, tree_count, 0)]
    mul x60 -> x0, other arithmetic: 41 us -> none  [the longest x30 20.6 us: combine(): second_scale[..., None] * second_out]
  transfers between devices with their start and end apart: 126 -> 0, of which waited for: 33 -> 0; matrix products, arithmetic and copies ran while one was open for 1% -> 0% of each run, Pallas kernels for 0% -> 0%
where the time goes in v3:
time: 125 us
  Pallas kernels  116 us (93%)
  local copies, waits for them, and re-layouts  6.15 us (5%)
  other arithmetic  3.35 us (3%)
    pallas_call x1, Pallas kernels, call(): pl.pallas_call(kernel, out_shape=jax.ShapeDtypeStruct((2, 128, 1024), BF)...  116 us
    unnamed x3, local copies, waits for them, and re-layouts  3.44 us

profile of v3, /device:TPU:0, one launch (start us, length us, event | category | flops | bytes accessed | tf_op | source)
XLA Modules:
  0.0 125.1 jit_solution(10929271350051074633)
XLA Ops:
  0.0 0.7 add_convert_fusion
  0.7 1.3 %convert_element_type.23 = f32[1,2048]{1,0:T(1,128)} convert(s32[1,2048]{1,0:T(1,128)} %param.22) | non-fusion elementwise | flops 2048 | bytes 16384 | tf_op jit(solution)/shard_map/convert_element_type | solution.py:580
  2.0 1.3 %broadcast_in_dim.2.gain = bf16[1,8192]{1,0:T(2,128)(2,1)} reshape(bf16[8192]{0:T(1024)(128)(2,1)} %param.13) | data formatting | bytes 32768 | tf_op jit(solution)/shard_map/broadcast_in_dim | solution.py:582
  3.3 0.8 copy.14
  4.1 0.1 reshape.40
  4.2 0.1 reshape.41
  4.3 0.6 pad.8.pages_in
  4.9 0.8 copy.16
  5.7 0.6 pad.9.fill
  6.3 0.5 fusion
  6.8 0.8 pad_maximum_fusion
  7.7 115.6 %shard_map.118 = bf16[2,128,1024]{2,1,0:T(8,128)(2,1)} custom-call(bf16[2,128,1024]{2,1,0:T(8,128)(2,1)} %hidden.1, bf16[1,8192]{1,0:T(2,128)(2,1)} %broadcast_in_dim.2.gain, f32[2,128,128]{2,1,0:T(8,128)} %get-tuple-element.8.cosine, f32[2,128,128]{2,1,0:T(8,128)} %get-tuple-element.9.sine, s32[2,8,128]{2,1,0:T(8,128)} %pad.8.pages_in, ...), custom_call_target="tpu_custom_call" | custom-call | flops 15000000512 | bytes 31457280 | tf_op jit(solution)/shard_map/pallas_call | solution.py:539
  123.3 1.9 %copy.18 = bf16[2,128,1024]{2,1,0:T(8,128)(2,1)} copy(bf16[2,128,1024]{2,1,0:T(8,128)(2,1)} %shard_map.118) | data formatting | bytes 1048576
  (3 shorter events, 0.0 us)

commit v4 on v3

v4 whole, which is shorter than its diff:
```python
import math

import jax
import jax.numpy as jnp
from jax import lax
from jax.experimental import pallas as pl
from jax.experimental.pallas import tpu as pltpu
from jax.sharding import PartitionSpec as P

MESH = pl.DeviceIdType.MESH
ROPE_BASE = 500000.0
EPSILON = 1e-05
LOW_SCORE = -1e30
LOW_MAX = -1e29
EXP_SCALE = math.log2(math.e) / math.sqrt(128.0)
BF, F32 = jnp.bfloat16, jnp.float32
CHUNKS = 2
ROWS = 128 // CHUNKS
TREES = 8 // CHUNKS
SPOTS = [(dy, dz) for dy in range(4) for dz in range(2)]
ORDER = [(0, 0), (1, 0), (3, 0), (0, 1), (2, 0), (1, 1), (3, 1), (2, 1)]


def kernel(
    hidden_hbm, gain_hbm, cosine_hbm, sine_hbm, pages_in, fill_hbm, depth_hbm, w_query, key_weight, value_weight,
    w_out_hbm, key_hbm, value_hbm,
    out,
    hidden, gain_in, gain, cosine, sine, fill, depth,
    held, sums, scale, weight, total, w_out, keys, values, filled, bias, bias_away, pages_away, pages,
    q_all, key_new, value_new, part, part_stat, got, got_stat, relay, relay_stat, rowed, rowed_stat, fresh, fresh_stat,
    vals, att, sent, got_y, got_z,
    send_sem, recv_sem, load_sem,
):
    c, h = lax.axis_index("cache"), lax.axis_index("head")
    x, zl, core = c // 4, lax.rem(c // 2, 2), lax.rem(c, 2)
    y, zh = h // 2, lax.rem(h, 2)

    def in_head(dy, dz):
        return lax.rem(y + dy, 4) * 2 + (zh if dz == 0 else 1 - zh)

    def in_cache(dx, dz):
        return lax.rem(x + dx, 4) * 4 + (zl if dz == 0 else 1 - zl) * 2 + core

    y_up, y_down, z_far = (c, in_head(1, 0)), (c, in_head(3, 0)), (c, in_head(0, 1))
    x_up, x_down, z_near = (in_cache(1, 0), h), (in_cache(3, 0), h), (in_cache(0, 1), h)
    twin = (c + 1 - 2 * core, h)

    loads = {}

    def load(name, src, dst):
        loads[name] = pltpu.make_async_copy(src, dst, load_sem.at[len(loads)])
        loads[name].start()

    def fetched(*names):
        for name in names:
            loads[name].wait()

    load("hidden", hidden_hbm, hidden)
    load("gain", gain_hbm, gain_in)
    load("pages", pages_in, pages.at[0])
    load("fill", fill_hbm, fill)
    load("depth", depth_hbm, depth)
    load("cosine", cosine_hbm, cosine)
    load("sine", sine_hbm, sine)
    for number, spot in enumerate(ORDER):
        rows = pl.ds(pl.multiple_of(in_head(*spot) * 1024, 1024), 1024)
        load(("q", number), w_query.at[rows], weight.at[number, :, pl.ds(0, 512)])
        load(("k", number), key_weight.at[rows], weight.at[number, :, pl.ds(512, 128)])
        load(("v", number), value_weight.at[rows], weight.at[number, :, pl.ds(640, 128)])
    load("keys", key_hbm, keys.at[pl.ds(0, 128)])
    load("values", value_hbm, values.at[pl.ds(0, 128)])
    load("out", w_out_hbm, w_out)

    barrier = pltpu.get_barrier_semaphore()
    others = [(c, in_head(*spot)) for spot in SPOTS[1:]] + [x_up, x_down, z_near, twin]
    for device in others:
        pl.semaphore_signal(barrier, inc=1, device_id=device, device_id_type=MESH)
    pl.semaphore_wait(barrier, len(others))

    made = {}

    def send(name, src, dst, device):
        number = len(made)
        made[name] = pltpu.make_async_remote_copy(
            src_ref=src, dst_ref=dst, send_sem=send_sem.at[number], recv_sem=recv_sem.at[number],
            device_id=device, device_id_type=MESH,
        )
        made[name].start()

    done = set()

    def arrived(*names):
        for name in names:
            if name not in done:
                done.add(name)
                made[name].wait_recv()


    def g_start(half, p):
        rows = pl.ds(half * ROWS, ROWS)
        for name, to, dy, dz in (("01", z_far, 0, 1), ("30", y_up, 3, 0), ("10", y_down, 1, 0)):
            send(f"a{half}{p}{name}", hidden_hbm.at[p, rows], held.at[half, dy, dz, p], to)

    low_rows, high_rows = pl.ds(0, ROWS // 2), pl.ds(ROWS // 2, ROWS // 2)

    def g_z(half):
        arrived(f"a{half}001")
        send(f"a{half}031", held.at[half, 0, 1, 0], held.at[half, 3, 1, 0], y_up)
        send(f"a{half}011", held.at[half, 0, 1, 0], held.at[half, 1, 1, 0], y_down)

    def g_up(half, p, dz):
        a = f"a{half}{p}"
        arrived(f"{a}3{dz}")
        if p == 1:
            send(f"a{half}131", held.at[half, 3, 0, 1], held.at[half, 3, 1, 1], z_far)
        send(f"{a}2{dz}u", held.at[half, 3, dz, p, low_rows], held.at[half, 2, dz, p, low_rows], y_up)

    def g_down(half, p, dz):
        a = f"a{half}{p}"
        arrived(f"{a}1{dz}")
        if p == 1:
            send(f"a{half}111", held.at[half, 1, 0, 1], held.at[half, 1, 1, 1], z_far)
        send(f"{a}2{dz}d", held.at[half, 1, dz, p, high_rows], held.at[half, 2, dz, p, high_rows], y_down)

    def g_far(half, n):
        rows = low_rows if n == "u" else high_rows
        arrived(f"a{half}120{n}")
        send(f"a{half}121{n}", held.at[half, 2, 0, 1, rows], held.at[half, 2, 1, 1, rows], z_far)

    ready = set()

    def multiply(half, dy, dz):
        number = ORDER.index((dy, dz))
        if number not in ready:
            for array in "qkv":
                fetched((array, number))
            ready.add(number)
        if (dy, dz) == (0, 0):
            rows = pl.ds(half * ROWS, ROWS)
            block = jnp.concatenate([hidden[0, rows], hidden[1, rows]], axis=0)
        else:
            for p in range(2):
                a = f"a{half}{p}{dy}{dz}"
                arrived(*([a + "u", a + "d"] if dy == 2 else [a]))
            block = held[half, dy, dz].reshape(2 * ROWS, 1024)
        normed = block.astype(F32) * scale[half][:, 0:1] * gain[in_head(dy, dz)]
        product = jnp.dot(normed.astype(BF), weight[number], preferred_element_type=F32)
        if (dy, dz) == (0, 0):
            total[half] = product
        else:
            total[half] += product

    def project_end(half):
        rows = pl.ds(half * ROWS, ROWS)
        cos = jnp.concatenate([cosine[0, rows], cosine[1, rows]], axis=0)
        sin = jnp.concatenate([sine[0, rows], sine[1, rows]], axis=0)
        cos, sin = jnp.concatenate([cos, cos], axis=1), jnp.concatenate([-sin, sin], axis=1)

        def turned(u):
            return (u * cos + pltpu.roll(u, 64, 1) * sin).astype(BF)

        k = turned(total[half, :, 512:640])
        v = total[half, :, 640:768].astype(BF)
        for head in range(4):
            q = turned(total[half, :, head * 128 : (head + 1) * 128])
            for p in range(2):
                for u in range(TREES):
                    low = (p * 4 + head) * 16
                    q_all[0, 0, half, u, low : low + 16] = q[p * ROWS + u * 16 : p * ROWS + u * 16 + 16]
        for p in range(2):
            for u in range(TREES):
                low, there = p * ROWS + u * 16, u * 32 + p * 16
                key_new[half, there : there + 16] = k[low : low + 16]
                value_new[half, there : there + 16, 0:128] = v[low : low + 16]
        name = f"q{half}"
        send(name + "30", q_all.at[0, 0, half], q_all.at[3, 0, half], x_up)
        send(name + "10", q_all.at[0, 0, half], q_all.at[1, 0, half], x_down)
        send(name + "01", q_all.at[0, 0, half], q_all.at[0, 1, half], z_near)


    def q_up(half, dz):
        q, trees = f"q{half}", pl.ds(0, TREES // 2)
        arrived(f"{q}3{dz}")
        send(f"{q}2{dz}u", q_all.at[3, dz, half, trees], q_all.at[2, dz, half, trees], x_up)

    def q_down(half, dz):
        q, trees = f"q{half}", pl.ds(TREES // 2, TREES // 2)
        arrived(f"{q}1{dz}")
        send(f"{q}2{dz}d", q_all.at[1, dz, half, trees], q_all.at[2, dz, half, trees], x_down)

    def q_z(half):
        q = f"q{half}"
        arrived(q + "01")
        send(q + "31", q_all.at[0, 1, half], q_all.at[3, 1, half], x_up)
        send(q + "11", q_all.at[0, 1, half], q_all.at[1, 1, half], x_down)


    lane = lax.broadcasted_iota(jnp.int32, (128, 128), 1)
    new_lane = lax.broadcasted_iota(jnp.int32, (128, TREES * 32), 1)
    new_row = lax.broadcasted_iota(jnp.int32, (128, TREES * 32), 0)

    def fresh_tokens(half):
        stats = jnp.zeros((128, 128), F32)
        for u in range(TREES):
            seen = (new_lane // 32 == u) & (new_lane % 16 == new_row % 16)
            seen = seen & ((new_lane % 32) // 16 <= new_row // 64)
            s = lax.dot_general(
                q_all[0, 0, half, u], key_new[half], (((1,), (1,)), ((), ())), preferred_element_type=F32
            )
            s = jnp.where(seen, s, LOW_SCORE)
            m = jnp.max(s, axis=1, keepdims=True)
            p = jnp.exp2((s - m) * EXP_SCALE).astype(BF)
            o = jnp.dot(p, value_new[half], preferred_element_type=F32)
            fresh[half, u] = o[:, 0:128].astype(BF)
            stats = jnp.where(lane == u, m, stats)
            stats = jnp.where(lane == u + 4, o[:, 128:256], stats)
        fresh_stat[half] = jnp.transpose(stats)[0:8]

    def block(half, dx, dz):
        owner = lax.rem(x + dx, 4) * 2 + (zl if dz == 0 else 1 - zl)
        if (dx, dz) != (0, 0):
            q = f"q{half}{dx}{dz}"
            arrived(*([q + "u", q + "d"] if dx == 2 else [q]))
        stats = jnp.zeros((128, 128), F32)
        for u in range(TREES):
            tree = owner * 8 + half * TREES + u
            among = (owner * 2 + core) * 8 + half * TREES + u
            numbers = [pages[b, i, among] + b * 128 for b in range(2) for i in range(8)]
            k = jnp.concatenate([keys[n] for n in numbers], axis=0)
            s = lax.dot_general(
                q_all[dx, dz, half, u], k, (((1,), (1,)), ((), ())), preferred_element_type=F32
            )
            hide = jnp.concatenate([bias[0, tree], bias[1, tree]], axis=1).astype(F32)
            s = jnp.concatenate([s[i * 16 : (i + 1) * 16] + hide for i in range(8)], axis=0)
            m = jnp.maximum(jnp.max(s, axis=1, keepdims=True), LOW_MAX)
            p = jnp.exp2((s - m) * EXP_SCALE).astype(BF)
            for i in range(16):
                vals[u, i * 64 : (i + 1) * 64, 0:128] = values[numbers[i]]
            o = jnp.dot(p, vals[u], preferred_element_type=F32)
            part[dx, dz, half, u] = o[:, 0:128].astype(BF)
            stats = jnp.where(lane == u, m, stats)
            stats = jnp.where(lane == u + 4, o[:, 128:256], stats)
        part_stat[dx, dz, half] = jnp.transpose(stats)[0:8]
        if dx == 2:
            send_part(half, 2, dz, relay.at[dz, half], relay_stat.at[dz, half], x_up if dz == 0 else x_down)
        if (dx, dz) == (1, 1):
            send_part(half, 1, 1, got.at[0, 1, half], got_stat.at[0, 1, half], x_up)
        if (dx, dz) == (3, 0):
            send_part(half, 3, 0, got.at[1, 0, half], got_stat.at[1, 0, half], x_down)

    def send_part(half, dx, dz, to, to_stat, device):
        send(f"o{half}{dx}{dz}", part.at[dx, dz, half], to, device)
        send(f"s{half}{dx}{dz}", part_stat.at[dx, dz, half], to_stat, device)

    def c_join(half, dz):
        arrived(f"o{half}2{dz}", f"s{half}2{dz}")
        dx = 1 if dz == 0 else 3
        outs = [part.at[dx, dz, half], relay.at[dz, half]]
        top, weights, summed = weigh([part_stat[dx, dz, half], relay_stat[dz, half]])
        columns = columns_of(weights)
        for u in range(TREES):
            part[dx, dz, half, u] = mixed(columns, outs, u).astype(BF)
        part_stat[dx, dz, half] = jnp.concatenate([top, summed], axis=0)
        slot = 0 if dz == 0 else 1
        send_part(half, dx, dz, got.at[slot, dz, half], got_stat.at[slot, dz, half], x_up if dz == 0 else x_down)

    def weigh(stats):
        tops = [s[0:4] for s in stats]
        top = tops[0]
        for other in tops[1:]:
            top = jnp.maximum(top, other)
        weights = [jnp.exp2((m - top) * EXP_SCALE) for m in tops]
        summed = jnp.zeros((4, 128), F32)
        for w, s in zip(weights, stats):
            summed = summed + w * s[4:8]
        return top, weights, summed

    def columns_of(weights):
        stacked = jnp.concatenate(weights + [jnp.zeros((128 - 4 * len(weights), 128), F32)], axis=0)
        return jnp.transpose(stacked)

    def mixed(columns, outs, u):
        o = jnp.zeros((128, 128), F32)
        for i, ref in enumerate(outs):
            o = o + columns[:, i * 4 + u : i * 4 + u + 1] * ref[u].astype(F32)
        return o

    def received(half, dz):
        arrived(*[f"{a}{half}{dx}{dz}" for a in "os" for dx in (1, 3)])
        outs = [part.at[0, dz, half]] + [got.at[i, dz, half] for i in range(2)]
        return outs, [part_stat[0, dz, half]] + [got_stat[i, dz, half] for i in range(2)]

    def plane_merge(half):
        outs, stats = received(half, 1)
        top, weights, summed = weigh(stats)
        columns = columns_of(weights)
        for u in range(TREES):
            rowed[0, half, u] = mixed(columns, outs, u).astype(BF)
        rowed_stat[0, half] = jnp.concatenate([top, summed], axis=0)
        send(f"zo{half}", rowed.at[0, half], rowed.at[1, half], z_near)
        send(f"zs{half}", rowed_stat.at[0, half], rowed_stat.at[1, half], z_near)

    def last_merge(half):
        outs, stats = received(half, 0)
        arrived(f"zo{half}", f"zs{half}")
        top, weights, summed = weigh(stats + [rowed_stat[1, half], fresh_stat[half]])
        columns = columns_of([w / summed for w in weights])
        for u in range(TREES):
            o = mixed(columns, outs + [rowed.at[1, half], fresh.at[half]], u).astype(BF)
            for p in range(2):
                for head in range(4):
                    low, there = (p * 4 + head) * 16, p * ROWS + u * 16
                    att[half, there : there + 16, head * 128 : (head + 1) * 128] = o[low : low + 16]


    rings = {"p": (0, 0, 1), "q": (1, 0, 0), "r": (2, 1, 0)}

    def product(half, dy, dz):
        if "out" not in done:
            done.add("out")
            fetched("out")
        features = pl.ds(pl.multiple_of(in_head(dy, dz) * 1024, 1024), 1024)
        r = jnp.dot(att[half], w_out[:, features], preferred_element_type=F32).astype(BF)
        sent[half, dz, dy] = r.reshape(2, ROWS, 1024)

    def over_z(half, dy):
        send(f"z{half}{dy}", sent.at[half, 1, dy, 1], got_z.at[half, dy], z_far)

    def add_z(half, dy):
        arrived(f"z{half}{dy}")
        sent[half, 0, dy, 1] = (sent[half, 0, dy, 1].astype(F32) + got_z[half, dy].astype(F32)).astype(BF)

    def ring_far(half, name):
        ring, p, dz = rings[name]
        for rows, to, n in ((low_rows, y_up, "u"), (high_rows, y_down, "d")):
            send(f"{name}f{half}{n}", sent.at[half, dz, 2, p, rows], got_y.at[half, ring, 0, rows], to)

    def ring_near(half, name, dy):
        ring, p, dz = rings[name]
        rows, to, n, slot = (high_rows, y_up, "u", 2) if dy == 1 else (low_rows, y_down, "d", 1)
        send(f"{name}n{half}{n}", sent.at[half, dz, dy, p, rows], got_y.at[half, ring, slot, rows], to)

    def d_join(half, name, dy):
        ring, p, dz = rings[name]
        rows, to, n, slot = (low_rows, y_up, "u", 2) if dy == 1 else (high_rows, y_down, "d", 1)
        arrived(f"{name}f{half}{n}")
        summed = sent[half, dz, dy, p, rows].astype(F32) + got_y[half, ring, 0, rows].astype(F32)
        sent[half, dz, dy, p, rows] = summed.astype(BF)
        send(f"{name}j{half}{n}", sent.at[half, dz, dy, p, rows], got_y.at[half, ring, slot, rows], to)

    def ring_end(half, name):
        ring, p, dz = rings[name]
        arrived(*[f"{name}{s}{half}{n}" for s in "nj" for n in "ud"])
        r = sent[half, dz, 0, p].astype(F32)
        return r + got_y[half, ring, 1].astype(F32) + got_y[half, ring, 2].astype(F32)

    def d_far(half, dz):
        product(half, 2, dz)
        ring_far(half, "p" if dz else "q")
        if dz:
            over_z(half, 2)

    def d_near(half, dy, dz):
        product(half, dy, dz)
        if dz:
            over_z(half, dy)
        ring_near(half, "p" if dz else "q", dy)

    def d_own(half, dz):
        product(half, 0, dz)
        if dz:
            over_z(half, 0)

    def r_far(half):
        add_z(half, 2)
        ring_far(half, "r")

    def r_near(half, dy):
        add_z(half, dy)
        ring_near(half, "r", dy)

    def d_cross(half):
        sent[half, 1, 0, 0] = ring_end(half, "p").astype(BF)
        send(f"y{half}", sent.at[half, 1, 0, 0], got_z.at[half, 4], z_far)

    def d_end(half, p):
        rows = pl.ds(half * ROWS, ROWS)
        if p == 0:
            first = ring_end(half, "q")
            arrived(f"y{half}")
            out[0, rows] = (first + got_z[half, 4].astype(F32)).astype(BF)
        else:
            add_z(half, 0)
            out[1, rows] = ring_end(half, "r").astype(BF)


    def exchange_start():
        send("pages", pages_in, pages_away, twin)
        send("keys", key_hbm, keys.at[pl.ds(128, 128)], twin)
        send("values", value_hbm, values.at[pl.ds(128, 128)], twin)

    def squares_start():
        fetched("hidden")
        fetched("gain")
        for i in range(64):
            gain[i // 8, :, i % 8 * 128 : i % 8 * 128 + 128] = gain_in[i : i + 1].astype(F32)
        for p in range(2):
            wide = hidden[p].astype(F32)
            squares = jnp.sum(wide * wide, axis=-1, keepdims=True)
            sums[0, 0, pl.ds(p, 1)] = jnp.transpose(jnp.broadcast_to(squares, (128, 128)))[0:1]
        for dy, dz in SPOTS[1:]:
            send(f"t{dy}{dz}", sums.at[0, 0], sums.at[(4 - dy) % 4, dz], (c, in_head(dy, dz)))

    def squares_end():
        arrived(*[f"t{dy}{dz}" for dy, dz in SPOTS[1:]])
        for p in range(2):
            s = sums[0, 0, pl.ds(p, 1)]
            for dy, dz in SPOTS[1:]:
                s = s + sums[dy, dz, pl.ds(p, 1)]
            s = jnp.transpose(jnp.broadcast_to(lax.rsqrt(s * (1.0 / 8192) + EPSILON), (128, 128)))
            for half in range(CHUNKS):
                scale[half, p * ROWS : (p + 1) * ROWS] = s[half * ROWS : (half + 1) * ROWS]

    def visibility():
        slot_row = lax.broadcasted_iota(jnp.int32, (128, 512), 0)
        slot_lane = lax.broadcasted_iota(jnp.int32, (128, 512), 1) // 64
        spread = jnp.where(slot_row == slot_lane, 1.0, 0.0).astype(BF)
        fetched("fill")
        fetched("depth")
        fills_t = jnp.concatenate([fill[...].astype(F32), jnp.zeros((120, 128), F32)], axis=0)
        filled[...] = jnp.dot(jnp.transpose(fills_t).astype(BF), spread, preferred_element_type=F32)
        column = lax.broadcasted_iota(jnp.int32, (16, 512), 1)
        slot_of, token_of = (column // 64).astype(F32), (column % 64).astype(F32)

        def group(target, j, e):
            depth_row = depth[:, pl.ds(pl.multiple_of(e * 128, 128), 128)].astype(F32)
            depths = jnp.transpose(jnp.broadcast_to(depth_row, (128, 128)))
            fills = filled[pl.ds(pl.multiple_of(e * 8, 8), 8)]
            for t in range(8):
                d = jnp.concatenate([depths[t * 16 : t * 16 + 16]] * 4, axis=1)
                visible = (slot_of < d) & (token_of < fills[t : t + 1])
                target[j * 8 + t] = jnp.where(visible, 0.0, LOW_SCORE).astype(BF)

        def away(j, _):
            group(bias_away, j, j * 2 + 1 - core)
            return 0

        def here(j, _):
            group(bias.at[0], j, j * 2 + core)
            return 0

        lax.fori_loop(0, 8, away, 0)
        send("bias", bias_away, bias.at[1], twin)
        lax.fori_loop(0, 8, here, 0)

    def exchange_end():
        arrived("pages")
        load("pages_away", pages_away, pages.at[1])
        for u in range(TREES):
            vals[u, :, 128:256] = jnp.ones((1024, 128), BF)
        for half in range(CHUNKS):
            value_new[half, :, 128:256] = jnp.ones((TREES * 32, 128), BF)
        fetched("pages", "pages_away", "keys", "values", "cosine", "sine")
        arrived("keys", "values", "bias")

    g_start(0, 1)
    g_start(0, 0)
    g_start(1, 0)
    g_down(0, 1, 0)
    g_up(0, 1, 0)
    g_z(0)
    squares_start()
    exchange_start()
    visibility()
    exchange_end()
    g_far(0, "u")
    g_up(0, 0, 0)
    g_far(0, "d")
    g_down(0, 0, 0)
    g_up(0, 0, 1)
    g_down(0, 0, 1)
    g_start(1, 1)
    g_z(1)
    squares_end()
    multiply(0, 0, 0)
    multiply(0, 3, 1)
    multiply(0, 0, 1)
    multiply(0, 2, 0)
    multiply(0, 1, 1)
    multiply(0, 1, 0)
    multiply(0, 3, 0)
    multiply(0, 2, 1)
    project_end(0)
    g_down(1, 1, 0)
    g_up(1, 1, 0)
    g_down(1, 0, 0)
    q_down(0, 0)
    q_z(0)
    g_up(1, 0, 0)
    g_down(1, 0, 1)
    g_far(1, "d")
    q_up(0, 0)
    block(0, 0, 0)
    g_up(1, 0, 1)
    block(0, 3, 0)
    g_far(1, "u")
    multiply(1, 0, 0)
    multiply(1, 3, 0)
    multiply(1, 2, 0)
    multiply(1, 1, 1)
    multiply(1, 1, 0)
    multiply(1, 3, 1)
    multiply(1, 0, 1)
    q_up(0, 1)
    q_down(0, 1)
    block(0, 2, 0)
    multiply(1, 2, 1)
    project_end(1)
    fresh_tokens(1)
    block(0, 2, 1)
    block(0, 1, 1)
    q_z(1)
    block(0, 3, 1)
    c_join(0, 1)
    block(0, 1, 0)
    c_join(0, 0)
    q_down(1, 0)
    q_up(1, 1)
    q_down(1, 1)
    q_up(1, 0)
    block(0, 0, 1)
    plane_merge(0)
    fresh_tokens(0)
    block(1, 1, 1)
    block(1, 2, 1)
    block(1, 2, 0)
    last_merge(0)
    d_near(0, 1, 1)
    d_near(0, 3, 0)
    d_far(0, 0)
    d_near(0, 1, 0)
    d_own(0, 0)
    d_near(0, 3, 1)
    d_far(0, 1)
    d_own(0, 1)
    block(1, 3, 1)
    c_join(1, 1)
    block(1, 1, 0)
    block(1, 0, 1)
    c_join(1, 0)
    d_join(0, "p", 1)
    d_join(0, "p", 3)
    block(1, 3, 0)
    plane_merge(1)
    r_far(0)
    d_join(0, "q", 1)
    d_cross(0)
    block(1, 0, 0)
    d_join(0, "q", 3)
    r_near(0, 1)
    d_join(0, "r", 1)
    r_near(0, 3)
    d_join(0, "r", 3)
    last_merge(1)
    d_far(1, 1)
    d_far(1, 0)
    d_near(1, 1, 0)
    d_near(1, 1, 1)
    d_near(1, 3, 1)
    d_join(1, "p", 3)
    d_join(1, "p", 1)
    d_near(1, 3, 0)
    r_far(1)
    d_join(1, "q", 3)
    d_join(1, "q", 1)
    d_own(1, 1)
    d_cross(1)
    r_near(1, 1)
    d_join(1, "r", 1)
    r_near(1, 3)
    d_join(1, "r", 3)
    d_end(0, 0)
    d_end(0, 1)
    d_own(1, 0)
    d_end(1, 0)
    d_end(1, 1)
    for copy in made.values():
        copy.wait_send()


def call(*operands):
    vm = pl.BlockSpec(memory_space=pltpu.VMEM)
    anywhere = pl.BlockSpec(memory_space=pl.ANY)
    n, r = CHUNKS, ROWS
    trees, tile = (n, TREES, 128, 128), (8, 128)
    stat = (n,) + tile
    shapes = [
        ((2, 128, 1024), BF), ((64, 128), BF), ((8, 1, 1024), F32), ((2, 128, 64), F32), ((2, 128, 64), F32),
        (tile, jnp.int32), ((1, 2048), jnp.int32),
        ((n, 4, 2, 2, r, 1024), BF), ((4, 2) + tile, F32), ((n, 2 * r, 128), F32), ((8, 1024, 768), BF),
        ((n, 2 * r, 768), F32), ((512, 8192), BF), ((256, 64, 128), BF), ((256, 64, 128), BF), ((128, 512), F32),
        ((2, 64, 16, 512), BF), ((64, 16, 512), BF), (tile, jnp.int32), None,
        ((4, 2) + trees, BF), ((n, TREES * 32, 128), BF), ((n, TREES * 32, 256), BF),
        ((4, 2) + trees, BF), ((4, 2) + stat, F32), ((2, 2) + trees, BF), ((2, 2) + stat, F32),
        ((2,) + trees, BF), ((2,) + stat, F32), ((2,) + trees, BF), ((2,) + stat, F32),
        (trees, BF), (stat, F32),
        ((TREES, 1024, 256), BF), ((n, 2 * r, 512), BF), ((n, 2, 4, 2, r, 1024), BF), ((n, 3, 3, r, 1024), BF),
        ((n, 5, r, 1024), BF),
    ]
    scratch = [pltpu.VMEM(*s) if s else pltpu.SMEM((2, 8, 128), jnp.int32) for s in shapes]
    return pl.pallas_call(
        kernel,
        out_shape=jax.ShapeDtypeStruct((2, 128, 1024), BF),
        in_specs=[anywhere] * 13,
        out_specs=vm,
        scratch_shapes=scratch
        + [pltpu.SemaphoreType.DMA((166,)), pltpu.SemaphoreType.DMA((166,)), pltpu.SemaphoreType.DMA((40,))],
        compiler_params=pltpu.CompilerParams(
            collective_id=1, has_side_effects=True, vmem_limit_bytes=61 * 2**20
        ),
        cost_estimate=pl.CostEstimate(flops=15 * 10**9, bytes_accessed=30 * 2**20, transcendentals=10**7),
    )(*operands)


def rope_tables(row_length):
    spots = row_length[None, :] + jnp.arange(2, dtype=jnp.int32)[:, None]
    ladder = jnp.arange(64, dtype=F32) * (2.0 / 128)
    frequency = jnp.power(jnp.float32(ROPE_BASE), -ladder)
    angles = spots.astype(F32)[..., None] * frequency
    cosine, sine = jnp.cos(angles), jnp.sin(angles)
    return cosine, sine


def body(
    hidden,
    norm_gain,
    w_query,
    key_weight,
    value_weight,
    w_out,
    key_cache,
    value_cache,
    tree_pages,
    page_fill,
    row_depth,
    row_length,
):
    cosine, sine = rope_tables(row_length)
    pages, fill = jnp.transpose(tree_pages[0]), jnp.transpose(page_fill[0])
    return call(
        hidden, norm_gain.reshape(64, 128), cosine, sine, pages, fill, row_depth, w_query, key_weight, value_weight, w_out,
        key_cache.reshape(128, 64, 128), value_cache.reshape(128, 64, 128),
    )


def solution(mesh):
    in_specs = (
        P(None, "cache", "head"),
        P(),
        P(None, "head"),
        P(None, "head"),
        P(None, "head"),
        P("head", None),
        P("cache", None, "head", None),
        P("cache", None, "head", None),
        P("cache", None, None),
        P("cache", None, None),
        P("cache", None),
        P("cache"),
    )
    out_specs = P(None, "cache", "head")
    return jax.shard_map(body, mesh=mesh, in_specs=in_specs, out_specs=out_specs, check_vma=False)
```

time: 125 us -> 107 us (0.86); the launches traced: 125 us -> 105 us
  Pallas kernels: 116 us -> 102 us
  local copies, waits for them, and re-layouts: 6.15 us -> 1.87 us
  other arithmetic: 3.35 us -> 1.91 us
    pallas_call x1, Pallas kernels: 116 us -> 102 us  [call(): pl.pallas_call(kernel, out_shape=jax.ShapeDtypeStruct((2, 128, 1024), BF)...]
    unnamed x3 -> x1, local copies, waits for them, and re-layouts: 3.44 us -> 1.87 us
    broadcast_in_dim x1 -> x0, local copies, waits for them, and re-layouts: 1.34 us -> none  [body(): norm_gain[None, :]]
    convert_element_type x2 -> x0, other arithmetic: 1.31 us -> none  [the longest x1 1.3 us: body(): depth = row_depth.reshape(16, 128).astype(F32)]
where the time goes in v4:
time: 107 us; the launch traced here: 105 us
  Pallas kernels  102 us (95%)
  other arithmetic  1.91 us (2%)
  local copies, waits for them, and re-layouts  1.87 us (2%)
    pallas_call x1, Pallas kernels, call(): pl.pallas_call(kernel, out_shape=jax.ShapeDtypeStruct((2, 128, 1024), BF)...  102 us

profile of v4, /device:TPU:0, one launch (start us, length us, event | category | flops | bytes accessed | tf_op | source)
XLA Modules:
  0.0 105.3 jit_solution(17062139470353452551)
XLA Ops:
  0.0 0.7 add_convert_fusion
  0.7 1.2 %multiply_sine_fusion = (f32[2,128,64]{2,1,0:T(8,128)}, f32[2,128,64]{2,1,0:T(8,128)}) fusion(f32[64]{0:T(128)S(1)} %negate_power_fusion, f32[2,128]{1,0:T(2,128)S(1)} %add_convert_fusion), kind=kLoop, calls=%fused_computation | loop fusion | flops 16384 | bytes 132352 | tf_op jit(solution)/shard_map/sin | solution.py:630
  1.9 101.5 %shard_map.118 = bf16[2,128,1024]{2,1,0:T(8,128)(2,1)} custom-call(bf16[2,128,1024]{2,1,0:T(8,128)(2,1)} %hidden_hbm.1, bf16[64,128]{1,0:T(8,128)(2,1)} %bitcast.11, f32[2,128,64]{2,1,0:T(8,128)} %get-tuple-element.6.cosine_hbm, f32[2,128,64]{2,1,0:T(8,128)} %get-tuple-element.5.sine_hbm, s32[8,128]{1,0:T(8,128)} %bitcast.12, s32[8,128]{1,0:T(8,128)} %bitcast.13, ...), custom_call_target="tpu_custom_call" | custom-call | flops 15000000512 | bytes 31457280 | tf_op jit(solution)/shard_map/pallas_call | solution.py:611
  103.4 1.9 %copy.14 = bf16[2,128,1024]{2,1,0:T(8,128)(2,1)} copy(bf16[2,128,1024]{2,1,0:T(8,128)(2,1)} %shard_map.118) | data formatting | bytes 1048576
  (1 shorter events, 0.0 us)

commit v5 on v4

--- a/solution.py
+++ b/solution.py
@@ -17,6 +17,7 @@
 CHUNKS = 2
 ROWS = 128 // CHUNKS
 TREES = 8 // CHUNKS
+FIRST = 80
 SPOTS = [(dy, dz) for dy in range(4) for dz in range(2)]
 ORDER = [(0, 0), (1, 0), (3, 0), (0, 1), (2, 0), (1, 1), (3, 1), (2, 1)]
 
@@ -25,9 +26,9 @@
     hidden_hbm, gain_hbm, cosine_hbm, sine_hbm, pages_in, fill_hbm, depth_hbm, w_query, key_weight, value_weight,
     w_out_hbm, key_hbm, value_hbm,
     out,
-    hidden, gain_in, gain, cosine, sine, fill, depth,
+    gain_in, gain, cosine, sine, fill, depth,
     held, sums, scale, weight, total, w_out, keys, values, filled, bias, bias_away, pages_away, pages,
-    q_all, key_new, value_new, part, part_stat, got, got_stat, relay, relay_stat, rowed, rowed_stat, fresh, fresh_stat,
+    q_all, key_new, value_new, part, part_stat, got, got_stat, relay, relay_stat, joined_stat, rowed, rowed_stat, fresh, fresh_stat,
     vals, att, sent, got_y, got_z,
     send_sem, recv_sem, load_sem,
 ):
@@ -55,7 +56,10 @@
         for name in names:
             loads[name].wait()
 
-    load("hidden", hidden_hbm, hidden)
+    for half in range(CHUNKS):
+        for p in range(2):
+            rows = pl.ds(half * ROWS, ROWS)
+            load(("own", half, p), hidden_hbm.at[p, rows], held.at[half, 0, 0, pl.ds(p * ROWS, ROWS)])
     load("gain", gain_hbm, gain_in)
     load("pages", pages_in, pages.at[0])
     load("fill", fill_hbm, fill)
@@ -78,6 +82,7 @@
     pl.semaphore_wait(barrier, len(others))
 
     made = {}
+    done = set()
 
     def send(name, src, dst, device):
         number = len(made)
@@ -87,8 +92,6 @@
         )
         made[name].start()
 
-    done = set()
-
     def arrived(*names):
         for name in names:
             if name not in done:
@@ -96,36 +99,40 @@
                 made[name].wait_recv()
 
 
+    group = (pl.ds(0, FIRST), pl.ds(FIRST, 2 * ROWS - FIRST))
+    ups = (pl.ds(0, 48), pl.ds(80, 16))
+    downs = (pl.ds(48, 32), pl.ds(96, 32))
+
     def g_start(half, p):
-        rows = pl.ds(half * ROWS, ROWS)
+        if ("own", half) not in done:
+            done.add(("own", half))
+            fetched(("own", half, 0), ("own", half, 1))
         for name, to, dy, dz in (("01", z_far, 0, 1), ("30", y_up, 3, 0), ("10", y_down, 1, 0)):
-            send(f"a{half}{p}{name}", hidden_hbm.at[p, rows], held.at[half, dy, dz, p], to)
-
-    low_rows, high_rows = pl.ds(0, ROWS // 2), pl.ds(ROWS // 2, ROWS // 2)
+            send(f"a{half}{p}{name}", held.at[half, 0, 0, group[p]], held.at[half, dy, dz, group[p]], to)
 
     def g_z(half):
         arrived(f"a{half}001")
-        send(f"a{half}031", held.at[half, 0, 1, 0], held.at[half, 3, 1, 0], y_up)
-        send(f"a{half}011", held.at[half, 0, 1, 0], held.at[half, 1, 1, 0], y_down)
+        send(f"a{half}031", held.at[half, 0, 1, group[0]], held.at[half, 3, 1, group[0]], y_up)
+        send(f"a{half}011", held.at[half, 0, 1, group[0]], held.at[half, 1, 1, group[0]], y_down)
 
     def g_up(half, p, dz):
         a = f"a{half}{p}"
         arrived(f"{a}3{dz}")
         if p == 1:
-            send(f"a{half}131", held.at[half, 3, 0, 1], held.at[half, 3, 1, 1], z_far)
-        send(f"{a}2{dz}u", held.at[half, 3, dz, p, low_rows], held.at[half, 2, dz, p, low_rows], y_up)
+            send(f"a{half}131", held.at[half, 3, 0, group[1]], held.at[half, 3, 1, group[1]], z_far)
+        send(f"{a}2{dz}u", held.at[half, 3, dz, ups[p]], held.at[half, 2, dz, ups[p]], y_up)
 
     def g_down(half, p, dz):
         a = f"a{half}{p}"
         arrived(f"{a}1{dz}")
         if p == 1:
-            send(f"a{half}111", held.at[half, 1, 0, 1], held.at[half, 1, 1, 1], z_far)
-        send(f"{a}2{dz}d", held.at[half, 1, dz, p, high_rows], held.at[half, 2, dz, p, high_rows], y_down)
+            send(f"a{half}111", held.at[half, 1, 0, group[1]], held.at[half, 1, 1, group[1]], z_far)
+        send(f"{a}2{dz}d", held.at[half, 1, dz, downs[p]], held.at[half, 2, dz, downs[p]], y_down)
 
     def g_far(half, n):
-        rows = low_rows if n == "u" else high_rows
+        rows = ups[1] if n == "u" else downs[1]
         arrived(f"a{half}120{n}")
-        send(f"a{half}121{n}", held.at[half, 2, 0, 1, rows], held.at[half, 2, 1, 1, rows], z_far)
+        send(f"a{half}121{n}", held.at[half, 2, 0, rows], held.at[half, 2, 1, rows], z_far)
 
     ready = set()
 
@@ -135,14 +142,11 @@
             for array in "qkv":
                 fetched((array, number))
             ready.add(number)
-        if (dy, dz) == (0, 0):
-            rows = pl.ds(half * ROWS, ROWS)
-            block = jnp.concatenate([hidden[0, rows], hidden[1, rows]], axis=0)
-        else:
+        if (dy, dz) != (0, 0):
             for p in range(2):
                 a = f"a{half}{p}{dy}{dz}"
                 arrived(*([a + "u", a + "d"] if dy == 2 else [a]))
-            block = held[half, dy, dz].reshape(2 * ROWS, 1024)
+        block = held[half, dy, dz]
         normed = block.astype(F32) * scale[half][:, 0:1] * gain[in_head(dy, dz)]
         product = jnp.dot(normed.astype(BF), weight[number], preferred_element_type=F32)
         if (dy, dz) == (0, 0):
@@ -178,15 +182,20 @@
         send(name + "01", q_all.at[0, 0, half], q_all.at[0, 1, half], z_near)
 
 
-    def q_up(half, dz):
-        q, trees = f"q{half}", pl.ds(0, TREES // 2)
-        arrived(f"{q}3{dz}")
-        send(f"{q}2{dz}u", q_all.at[3, dz, half, trees], q_all.at[2, dz, half, trees], x_up)
-
-    def q_down(half, dz):
-        q, trees = f"q{half}", pl.ds(TREES // 2, TREES // 2)
-        arrived(f"{q}1{dz}")
-        send(f"{q}2{dz}d", q_all.at[1, dz, half, trees], q_all.at[2, dz, half, trees], x_down)
+    low_trees, high_trees = pl.ds(0, TREES // 2), pl.ds(TREES // 2, TREES // 2)
+
+    def q_up(half):
+        arrived(f"q{half}30")
+        send(f"q{half}20u", q_all.at[3, 0, half, low_trees], q_all.at[2, 0, half, low_trees], x_up)
+
+    def q_down(half):
+        arrived(f"q{half}10")
+        send(f"q{half}20d", q_all.at[1, 0, half, high_trees], q_all.at[2, 0, half, high_trees], x_down)
+
+    def q_cross(half, n):
+        trees = low_trees if n == "u" else high_trees
+        arrived(f"q{half}20{n}")
+        send(f"q{half}21{n}", q_all.at[2, 0, half, trees], q_all.at[2, 1, half, trees], z_near)
 
     def q_z(half):
         q = f"q{half}"
@@ -248,21 +257,30 @@
         if (dx, dz) == (3, 0):
             send_part(half, 3, 0, got.at[1, 0, half], got_stat.at[1, 0, half], x_down)
 
+    def send_trees(name, k, src, dst, device):
+        trees = low_trees if k == 0 else high_trees
+        send(f"{name}{k}", src.at[trees], dst.at[trees], device)
+
     def send_part(half, dx, dz, to, to_stat, device):
-        send(f"o{half}{dx}{dz}", part.at[dx, dz, half], to, device)
         send(f"s{half}{dx}{dz}", part_stat.at[dx, dz, half], to_stat, device)
-
-    def c_join(half, dz):
-        arrived(f"o{half}2{dz}", f"s{half}2{dz}")
-        dx = 1 if dz == 0 else 3
+        for k in range(2):
+            send_trees(f"o{half}{dx}{dz}", k, part.at[dx, dz, half], to, device)
+
+    def some_trees(k):
+        return range(k * TREES // 2, (k + 1) * TREES // 2)
+
+    def c_join(half, dz, k):
+        arrived(f"o{half}2{dz}{k}", f"s{half}2{dz}")
+        dx, slot, device = (1, 0, x_up) if dz == 0 else (3, 1, x_down)
         outs = [part.at[dx, dz, half], relay.at[dz, half]]
         top, weights, summed = weigh([part_stat[dx, dz, half], relay_stat[dz, half]])
         columns = columns_of(weights)
-        for u in range(TREES):
+        if k == 0:
+            joined_stat[dz, half] = jnp.concatenate([top, summed], axis=0)
+            send(f"s{half}{dx}{dz}", joined_stat.at[dz, half], got_stat.at[slot, dz, half], device)
+        for u in some_trees(k):
             part[dx, dz, half, u] = mixed(columns, outs, u).astype(BF)
-        part_stat[dx, dz, half] = jnp.concatenate([top, summed], axis=0)
-        slot = 0 if dz == 0 else 1
-        send_part(half, dx, dz, got.at[slot, dz, half], got_stat.at[slot, dz, half], x_up if dz == 0 else x_down)
+        send_trees(f"o{half}{dx}{dz}", k, part.at[dx, dz, half], got.at[slot, dz, half], device)
 
     def weigh(stats):
         tops = [s[0:4] for s in stats]
@@ -285,27 +303,29 @@
             o = o + columns[:, i * 4 + u : i * 4 + u + 1] * ref[u].astype(F32)
         return o
 
-    def received(half, dz):
-        arrived(*[f"{a}{half}{dx}{dz}" for a in "os" for dx in (1, 3)])
+    def received(half, dz, k):
+        for dx in (1, 3):
+            arrived(f"s{half}{dx}{dz}", f"o{half}{dx}{dz}{k}")
         outs = [part.at[0, dz, half]] + [got.at[i, dz, half] for i in range(2)]
         return outs, [part_stat[0, dz, half]] + [got_stat[i, dz, half] for i in range(2)]
 
-    def plane_merge(half):
-        outs, stats = received(half, 1)
+    def plane_merge(half, k):
+        outs, stats = received(half, 1, k)
         top, weights, summed = weigh(stats)
         columns = columns_of(weights)
-        for u in range(TREES):
+        if k == 0:
+            rowed_stat[0, half] = jnp.concatenate([top, summed], axis=0)
+            send(f"zs{half}", rowed_stat.at[0, half], rowed_stat.at[1, half], z_near)
+        for u in some_trees(k):
             rowed[0, half, u] = mixed(columns, outs, u).astype(BF)
-        rowed_stat[0, half] = jnp.concatenate([top, summed], axis=0)
-        send(f"zo{half}", rowed.at[0, half], rowed.at[1, half], z_near)
-        send(f"zs{half}", rowed_stat.at[0, half], rowed_stat.at[1, half], z_near)
-
-    def last_merge(half):
-        outs, stats = received(half, 0)
-        arrived(f"zo{half}", f"zs{half}")
+        send_trees(f"zo{half}", k, rowed.at[0, half], rowed.at[1, half], z_near)
+
+    def last_merge(half, k):
+        outs, stats = received(half, 0, k)
+        arrived(f"zs{half}", f"zo{half}{k}")
         top, weights, summed = weigh(stats + [rowed_stat[1, half], fresh_stat[half]])
         columns = columns_of([w / summed for w in weights])
-        for u in range(TREES):
+        for u in some_trees(k):
             o = mixed(columns, outs + [rowed.at[1, half], fresh.at[half]], u).astype(BF)
             for p in range(2):
                 for head in range(4):
@@ -321,38 +341,40 @@
             fetched("out")
         features = pl.ds(pl.multiple_of(in_head(dy, dz) * 1024, 1024), 1024)
         r = jnp.dot(att[half], w_out[:, features], preferred_element_type=F32).astype(BF)
-        sent[half, dz, dy] = r.reshape(2, ROWS, 1024)
+        sent[half, dz, dy] = r
 
     def over_z(half, dy):
-        send(f"z{half}{dy}", sent.at[half, 1, dy, 1], got_z.at[half, dy], z_far)
+        send(f"z{half}{dy}", sent.at[half, 1, dy, group[1]], got_z.at[half, dy, group[1]], z_far)
 
     def add_z(half, dy):
         arrived(f"z{half}{dy}")
-        sent[half, 0, dy, 1] = (sent[half, 0, dy, 1].astype(F32) + got_z[half, dy].astype(F32)).astype(BF)
+        rows = group[1]
+        sent[half, 0, dy, rows] = (sent[half, 0, dy, rows].astype(F32) + got_z[half, dy, rows].astype(F32)).astype(BF)
 
     def ring_far(half, name):
         ring, p, dz = rings[name]
-        for rows, to, n in ((low_rows, y_up, "u"), (high_rows, y_down, "d")):
-            send(f"{name}f{half}{n}", sent.at[half, dz, 2, p, rows], got_y.at[half, ring, 0, rows], to)
+        for rows, to, n in ((ups[p], y_up, "u"), (downs[p], y_down, "d")):
+            send(f"{name}f{half}{n}", sent.at[half, dz, 2, rows], got_y.at[half, ring, 0, rows], to)
 
     def ring_near(half, name, dy):
         ring, p, dz = rings[name]
-        rows, to, n, slot = (high_rows, y_up, "u", 2) if dy == 1 else (low_rows, y_down, "d", 1)
-        send(f"{name}n{half}{n}", sent.at[half, dz, dy, p, rows], got_y.at[half, ring, slot, rows], to)
+        rows, to, n, slot = (downs[p], y_up, "u", 2) if dy == 1 else (ups[p], y_down, "d", 1)
+        send(f"{name}n{half}{n}", sent.at[half, dz, dy, rows], got_y.at[half, ring, slot, rows], to)
 
     def d_join(half, name, dy):
         ring, p, dz = rings[name]
-        rows, to, n, slot = (low_rows, y_up, "u", 2) if dy == 1 else (high_rows, y_down, "d", 1)
+        rows, to, n, slot = (ups[p], y_up, "u", 2) if dy == 1 else (downs[p], y_down, "d", 1)
         arrived(f"{name}f{half}{n}")
-        summed = sent[half, dz, dy, p, rows].astype(F32) + got_y[half, ring, 0, rows].astype(F32)
-        sent[half, dz, dy, p, rows] = summed.astype(BF)
-        send(f"{name}j{half}{n}", sent.at[half, dz, dy, p, rows], got_y.at[half, ring, slot, rows], to)
+        summed = sent[half, dz, dy, rows].astype(F32) + got_y[half, ring, 0, rows].astype(F32)
+        sent[half, dz, dy, rows] = summed.astype(BF)
+        send(f"{name}j{half}{n}", sent.at[half, dz, dy, rows], got_y.at[half, ring, slot, rows], to)
 
     def ring_end(half, name):
         ring, p, dz = rings[name]
         arrived(*[f"{name}{s}{half}{n}" for s in "nj" for n in "ud"])
-        r = sent[half, dz, 0, p].astype(F32)
-        return r + got_y[half, ring, 1].astype(F32) + got_y[half, ring, 2].astype(F32)
+        rows = group[p]
+        r = sent[half, dz, 0, rows].astype(F32)
+        return r + got_y[half, ring, 1, rows].astype(F32) + got_y[half, ring, 2, rows].astype(F32)
 
     def d_far(half, dz):
         product(half, 2, dz)
@@ -380,18 +402,20 @@
         ring_near(half, "r", dy)
 
     def d_cross(half):
-        sent[half, 1, 0, 0] = ring_end(half, "p").astype(BF)
-        send(f"y{half}", sent.at[half, 1, 0, 0], got_z.at[half, 4], z_far)
+        sent[half, 1, 0, group[0]] = ring_end(half, "p").astype(BF)
+        send(f"y{half}", sent.at[half, 1, 0, group[0]], got_z.at[half, 4, group[0]], z_far)
 
     def d_end(half, p):
-        rows = pl.ds(half * ROWS, ROWS)
+        low = half * ROWS
         if p == 0:
             first = ring_end(half, "q")
             arrived(f"y{half}")
-            out[0, rows] = (first + got_z[half, 4].astype(F32)).astype(BF)
+            first = (first + got_z[half, 4, group[0]].astype(F32)).astype(BF)
+            out[0, low : low + ROWS] = first[0:ROWS]
+            out[1, low : low + FIRST - ROWS] = first[ROWS:FIRST]
         else:
             add_z(half, 0)
-            out[1, rows] = ring_end(half, "r").astype(BF)
+            out[1, low + FIRST - ROWS : low + ROWS] = ring_end(half, "r").astype(BF)
 
 
     def exchange_start():
@@ -400,12 +424,16 @@
         send("values", value_hbm, values.at[pl.ds(128, 128)], twin)
 
     def squares_start():
-        fetched("hidden")
+        for half in range(CHUNKS):
+            if ("own", half) not in done:
+                done.add(("own", half))
+                fetched(("own", half, 0), ("own", half, 1))
         fetched("gain")
         for i in range(64):
             gain[i // 8, :, i % 8 * 128 : i % 8 * 128 + 128] = gain_in[i : i + 1].astype(F32)
         for p in range(2):
-            wide = hidden[p].astype(F32)
+            rows = slice(p * ROWS, (p + 1) * ROWS)
+            wide = jnp.concatenate([held[half, 0, 0, rows] for half in range(CHUNKS)], axis=0).astype(F32)
             squares = jnp.sum(wide * wide, axis=-1, keepdims=True)
             sums[0, 0, pl.ds(p, 1)] = jnp.transpose(jnp.broadcast_to(squares, (128, 128)))[0:1]
         for dy, dz in SPOTS[1:]:
@@ -463,127 +491,135 @@
         fetched("pages", "pages_away", "keys", "values", "cosine", "sine")
         arrived("keys", "values", "bias")
 
-    g_start(0, 1)
-    g_start(0, 0)
+    g_start(1, 1)
+    squares_start()
     g_start(1, 0)
-    g_down(0, 1, 0)
-    g_up(0, 1, 0)
-    g_z(0)
-    squares_start()
     exchange_start()
     visibility()
     exchange_end()
-    g_far(0, "u")
-    g_up(0, 0, 0)
-    g_far(0, "d")
-    g_down(0, 0, 0)
-    g_up(0, 0, 1)
-    g_down(0, 0, 1)
-    g_start(1, 1)
-    g_z(1)
+    g_down(1, 1, 0)
+    g_up(1, 1, 0)
     squares_end()
     multiply(0, 0, 0)
+    g_start(0, 1)
+    multiply(1, 0, 0)
+    g_z(1)
+    multiply(1, 3, 0)
+    multiply(1, 1, 0)
+    g_up(1, 0, 0)
+    g_down(1, 0, 0)
+    g_far(1, "u")
+    g_far(1, "d")
+    multiply(1, 0, 1)
+    g_up(1, 0, 1)
+    g_down(1, 0, 1)
+    g_start(0, 0)
+    g_down(0, 1, 0)
+    multiply(1, 1, 1)
+    multiply(1, 3, 1)
+    multiply(1, 2, 0)
+    multiply(1, 2, 1)
+    project_end(1)
+    g_up(0, 1, 0)
+    g_z(0)
+    multiply(0, 0, 1)
+    block(1, 0, 0)
+    g_far(0, "u")
+    g_far(0, "d")
+    g_up(0, 0, 0)
+    fresh_tokens(1)
+    g_down(0, 0, 0)
+    multiply(0, 3, 0)
+    q_up(1)
+    q_down(1)
+    multiply(0, 1, 0)
+    block(1, 3, 0)
+    g_up(0, 0, 1)
+    multiply(0, 1, 1)
+    g_down(0, 0, 1)
+    block(1, 0, 1)
+    q_cross(1, "d")
+    q_z(1)
     multiply(0, 3, 1)
-    multiply(0, 0, 1)
+    q_cross(1, "u")
     multiply(0, 2, 0)
-    multiply(0, 1, 1)
-    multiply(0, 1, 0)
-    multiply(0, 3, 0)
+    block(1, 1, 0)
     multiply(0, 2, 1)
     project_end(0)
-    g_down(1, 1, 0)
-    g_up(1, 1, 0)
-    g_down(1, 0, 0)
-    q_down(0, 0)
+    block(1, 2, 0)
+    block(1, 2, 1)
+    block(1, 3, 1)
+    fresh_tokens(0)
+    q_up(0)
+    q_down(0)
+    block(1, 1, 1)
+    c_join(1, 1, 0)
+    block(0, 0, 1)
+    c_join(1, 1, 1)
+    q_cross(0, "u")
     q_z(0)
-    g_up(1, 0, 0)
-    g_down(1, 0, 1)
-    g_far(1, "d")
-    q_up(0, 0)
-    block(0, 0, 0)
-    g_up(1, 0, 1)
-    block(0, 3, 0)
-    g_far(1, "u")
-    multiply(1, 0, 0)
-    multiply(1, 3, 0)
-    multiply(1, 2, 0)
-    multiply(1, 1, 1)
-    multiply(1, 1, 0)
-    multiply(1, 3, 1)
-    multiply(1, 0, 1)
-    q_up(0, 1)
-    q_down(0, 1)
+    q_cross(0, "d")
+    c_join(1, 0, 0)
+    c_join(1, 0, 1)
     block(0, 2, 0)
-    multiply(1, 2, 1)
-    project_end(1)
-    fresh_tokens(1)
+    plane_merge(1, 0)
+    plane_merge(1, 1)
+    block(0, 1, 0)
     block(0, 2, 1)
     block(0, 1, 1)
-    q_z(1)
+    last_merge(1, 0)
+    last_merge(1, 1)
+    d_far(1, 1)
+    d_near(1, 3, 1)
+    d_near(1, 1, 0)
     block(0, 3, 1)
-    c_join(0, 1)
-    block(0, 1, 0)
-    c_join(0, 0)
-    q_down(1, 0)
-    q_up(1, 1)
-    q_down(1, 1)
-    q_up(1, 0)
-    block(0, 0, 1)
-    plane_merge(0)
-    fresh_tokens(0)
-    block(1, 1, 1)
-    block(1, 2, 1)
-    block(1, 2, 0)
-    last_merge(0)
+    c_join(0, 1, 0)
+    c_join(0, 1, 1)
+    d_far(1, 0)
+    c_join(0, 0, 0)
+    c_join(0, 0, 1)
+    d_near(1, 1, 1)
+    d_join(1, "p", 1)
+    r_far(1)
+    d_join(1, "p", 3)
+    block(0, 3, 0)
+    plane_merge(0, 0)
+    plane_merge(0, 1)
+    d_near(1, 3, 0)
+    r_near(1, 3)
+    d_own(1, 0)
+    d_join(1, "r", 3)
+    d_join(1, "q", 1)
+    r_near(1, 1)
+    d_own(1, 1)
+    d_join(1, "q", 3)
+    block(0, 0, 0)
+    d_cross(1)
+    last_merge(0, 0)
+    d_join(1, "r", 1)
+    last_merge(0, 1)
+    d_own(0, 0)
+    d_far(0, 1)
     d_near(0, 1, 1)
-    d_near(0, 3, 0)
+    d_near(0, 3, 1)
     d_far(0, 0)
-    d_near(0, 1, 0)
-    d_own(0, 0)
-    d_near(0, 3, 1)
-    d_far(0, 1)
     d_own(0, 1)
-    block(1, 3, 1)
-    c_join(1, 1)
-    block(1, 1, 0)
-    block(1, 0, 1)
-    c_join(1, 0)
     d_join(0, "p", 1)
     d_join(0, "p", 3)
-    block(1, 3, 0)
-    plane_merge(1)
     r_far(0)
+    d_near(0, 3, 0)
+    d_join(0, "q", 3)
+    d_near(0, 1, 0)
+    d_end(1, 1)
+    r_near(0, 1)
+    d_cross(0)
+    d_end(1, 0)
+    d_join(0, "r", 1)
     d_join(0, "q", 1)
-    d_cross(0)
-    block(1, 0, 0)
-    d_join(0, "q", 3)
-    r_near(0, 1)
-    d_join(0, "r", 1)
     r_near(0, 3)
     d_join(0, "r", 3)
-    last_merge(1)
-    d_far(1, 1)
-    d_far(1, 0)
-    d_near(1, 1, 0)
-    d_near(1, 1, 1)
-    d_near(1, 3, 1)
-    d_join(1, "p", 3)
-    d_join(1, "p", 1)
-    d_near(1, 3, 0)
-    r_far(1)
-    d_join(1, "q", 3)
-    d_join(1, "q", 1)
-    d_own(1, 1)
-    d_cross(1)
-    r_near(1, 1)
-    d_join(1, "r", 1)
-    r_near(1, 3)
-    d_join(1, "r", 3)
+    d_end(0, 1)
     d_end(0, 0)
-    d_end(0, 1)
-    d_own(1, 0)
-    d_end(1, 0)
-    d_end(1, 1)
     for copy in made.values():
         copy.wait_send()
 
@@ -595,17 +631,17 @@
     trees, tile = (n, TREES, 128, 128), (8, 128)
     stat = (n,) + tile
     shapes = [
-        ((2, 128, 1024), BF), ((64, 128), BF), ((8, 1, 1024), F32), ((2, 128, 64), F32), ((2, 128, 64), F32),
+        ((64, 128), BF), ((8, 1, 1024), F32), ((2, 128, 64), F32), ((2, 128, 64), F32),
         (tile, jnp.int32), ((1, 2048), jnp.int32),
-        ((n, 4, 2, 2, r, 1024), BF), ((4, 2) + tile, F32), ((n, 2 * r, 128), F32), ((8, 1024, 768), BF),
+        ((n, 4, 2, 2 * r, 1024), BF), ((4, 2) + tile, F32), ((n, 2 * r, 128), F32), ((8, 1024, 768), BF),
         ((n, 2 * r, 768), F32), ((512, 8192), BF), ((256, 64, 128), BF), ((256, 64, 128), BF), ((128, 512), F32),
         ((2, 64, 16, 512), BF), ((64, 16, 512), BF), (tile, jnp.int32), None,
         ((4, 2) + trees, BF), ((n, TREES * 32, 128), BF), ((n, TREES * 32, 256), BF),
         ((4, 2) + trees, BF), ((4, 2) + stat, F32), ((2, 2) + trees, BF), ((2, 2) + stat, F32),
-        ((2,) + trees, BF), ((2,) + stat, F32), ((2,) + trees, BF), ((2,) + stat, F32),
+        ((2,) + trees, BF), ((2,) + stat, F32), ((2,) + stat, F32), ((2,) + trees, BF), ((2,) + stat, F32),
         (trees, BF), (stat, F32),
-        ((TREES, 1024, 256), BF), ((n, 2 * r, 512), BF), ((n, 2, 4, 2, r, 1024), BF), ((n, 3, 3, r, 1024), BF),
-        ((n, 5, r, 1024), BF),
+        ((TREES, 1024, 256), BF), ((n, 2 * r, 512), BF), ((n, 2, 4, 2 * r, 1024), BF),
+        ((n, 3, 3, 2 * r, 1024), BF), ((n, 5, 2 * r, 1024), BF),
     ]
     scratch = [pltpu.VMEM(*s) if s else pltpu.SMEM((2, 8, 128), jnp.int32) for s in shapes]
     return pl.pallas_call(
@@ -614,9 +650,9 @@
         in_specs=[anywhere] * 13,
         out_specs=vm,
         scratch_shapes=scratch
-        + [pltpu.SemaphoreType.DMA((166,)), pltpu.SemaphoreType.DMA((166,)), pltpu.SemaphoreType.DMA((40,))],
+        + [pltpu.SemaphoreType.DMA((196,)), pltpu.SemaphoreType.DMA((196,)), pltpu.SemaphoreType.DMA((40,))],
         compiler_params=pltpu.CompilerParams(
-            collective_id=1, has_side_effects=True, vmem_limit_bytes=61 * 2**20
+            collective_id=1, has_side_effects=True, vmem_limit_bytes=60 * 2**20
         ),
         cost_estimate=pl.CostEstimate(flops=15 * 10**9, bytes_accessed=30 * 2**20, transcendentals=10**7),
     )(*operands)

time: 107 us -> 102 us (0.953)
  Pallas kernels: 102 us -> 97.6 us
    pallas_call x1, Pallas kernels: 102 us -> 97.6 us  [call(): pl.pallas_call(kernel, out_shape=jax.ShapeDtypeStruct((2, 128, 1024), BF)...]
where the time goes in v5:
time: 102 us; the launch traced here: 101 us
  Pallas kernels  97.6 us (96%)
  other arithmetic  1.91 us (2%)
  local copies, waits for them, and re-layouts  1.87 us (2%)
    pallas_call x1, Pallas kernels, call(): pl.pallas_call(kernel, out_shape=jax.ShapeDtypeStruct((2, 128, 1024), BF)...  97.6 us

profile of v5, /device:TPU:0, one launch (start us, length us, event | category | flops | bytes accessed | tf_op | source)
XLA Modules:
  0.0 101.3 jit_solution(14725387283132515166)
XLA Ops:
  0.0 0.7 add_convert_fusion
  0.7 1.2 %multiply_sine_fusion = (f32[2,128,64]{2,1,0:T(8,128)}, f32[2,128,64]{2,1,0:T(8,128)}) fusion(f32[64]{0:T(128)S(1)} %negate_power_fusion, f32[2,128]{1,0:T(2,128)S(1)} %add_convert_fusion), kind=kLoop, calls=%fused_computation | loop fusion | flops 16384 | bytes 132352 | tf_op jit(solution)/shard_map/sin | solution.py:666
  1.9 97.6 %shard_map.118 = bf16[2,128,1024]{2,1,0:T(8,128)(2,1)} custom-call(bf16[2,128,1024]{2,1,0:T(8,128)(2,1)} %hidden_hbm.1, bf16[64,128]{1,0:T(8,128)(2,1)} %bitcast.11, f32[2,128,64]{2,1,0:T(8,128)} %get-tuple-element.6.cosine_hbm, f32[2,128,64]{2,1,0:T(8,128)} %get-tuple-element.5.sine_hbm, s32[8,128]{1,0:T(8,128)} %bitcast.12, s32[8,128]{1,0:T(8,128)} %bitcast.13, ...), custom_call_target="tpu_custom_call" | custom-call | flops 15000000512 | bytes 31457280 | tf_op jit(solution)/shard_map/pallas_call | solution.py:647
  99.5 1.9 %copy.14 = bf16[2,128,1024]{2,1,0:T(8,128)(2,1)} copy(bf16[2,128,1024]{2,1,0:T(8,128)(2,1)} %shard_map.118) | data formatting | bytes 1048576
  (1 shorter events, 0.0 us)

commit v6 on v5

--- a/solution.py
+++ b/solution.py
@@ -2,6 +2,7 @@
 
 import jax
 import jax.numpy as jnp
+import numpy as np
 from jax import lax
 from jax.experimental import pallas as pl
 from jax.experimental.pallas import tpu as pltpu
@@ -23,10 +24,10 @@
 
 
 def kernel(
-    hidden_hbm, gain_hbm, cosine_hbm, sine_hbm, pages_in, fill_hbm, depth_hbm, w_query, key_weight, value_weight,
+    hidden_hbm, gain_hbm, lengths_hbm, frequency_hbm, pages_in, fill_hbm, depth_hbm, w_query, key_weight, value_weight,
     w_out_hbm, key_hbm, value_hbm,
     out,
-    gain_in, gain, cosine, sine, fill, depth,
+    gain_in, gain, lengths, frequency, cosine, sine, fill, depth,
     held, sums, scale, weight, total, w_out, keys, values, filled, bias, bias_away, pages_away, pages,
     q_all, key_new, value_new, part, part_stat, got, got_stat, relay, relay_stat, joined_stat, rowed, rowed_stat, fresh, fresh_stat,
     vals, att, sent, got_y, got_z,
@@ -64,8 +65,8 @@
     load("pages", pages_in, pages.at[0])
     load("fill", fill_hbm, fill)
     load("depth", depth_hbm, depth)
-    load("cosine", cosine_hbm, cosine)
-    load("sine", sine_hbm, sine)
+    load("lengths", lengths_hbm, lengths)
+    load("frequency", frequency_hbm, frequency)
     for number, spot in enumerate(ORDER):
         rows = pl.ds(pl.multiple_of(in_head(*spot) * 1024, 1024), 1024)
         load(("q", number), w_query.at[rows], weight.at[number, :, pl.ds(0, 512)])
@@ -154,6 +155,8 @@
         else:
             total[half] += product
 
+    low_trees, high_trees = pl.ds(0, TREES // 2), pl.ds(TREES // 2, TREES // 2)
+
     def project_end(half):
         rows = pl.ds(half * ROWS, ROWS)
         cos = jnp.concatenate([cosine[0, rows], cosine[1, rows]], axis=0)
@@ -177,19 +180,20 @@
                 key_new[half, there : there + 16] = k[low : low + 16]
                 value_new[half, there : there + 16, 0:128] = v[low : low + 16]
         name = f"q{half}"
-        send(name + "30", q_all.at[0, 0, half], q_all.at[3, 0, half], x_up)
-        send(name + "10", q_all.at[0, 0, half], q_all.at[1, 0, half], x_down)
+        for first, there, trees, device in (
+            ("30l", 3, low_trees, x_up), ("10h", 1, high_trees, x_down),
+            ("30h", 3, high_trees, x_up), ("10l", 1, low_trees, x_down),
+        ):
+            send(name + first, q_all.at[0, 0, half, trees], q_all.at[there, 0, half, trees], device)
         send(name + "01", q_all.at[0, 0, half], q_all.at[0, 1, half], z_near)
 
 
-    low_trees, high_trees = pl.ds(0, TREES // 2), pl.ds(TREES // 2, TREES // 2)
-
     def q_up(half):
-        arrived(f"q{half}30")
+        arrived(f"q{half}30l")
         send(f"q{half}20u", q_all.at[3, 0, half, low_trees], q_all.at[2, 0, half, low_trees], x_up)
 
     def q_down(half):
-        arrived(f"q{half}10")
+        arrived(f"q{half}10h")
         send(f"q{half}20d", q_all.at[1, 0, half, high_trees], q_all.at[2, 0, half, high_trees], x_down)
 
     def q_cross(half, n):
@@ -229,7 +233,7 @@
         owner = lax.rem(x + dx, 4) * 2 + (zl if dz == 0 else 1 - zl)
         if (dx, dz) != (0, 0):
             q = f"q{half}{dx}{dz}"
-            arrived(*([q + "u", q + "d"] if dx == 2 else [q]))
+            arrived(*(q + n for n in ("ud" if dx == 2 else "lh" if dz == 0 else [""])))
         stats = jnp.zeros((128, 128), F32)
         for u in range(TREES):
             tree = owner * 8 + half * TREES + u
@@ -333,7 +337,7 @@
                     att[half, there : there + 16, head * 128 : (head + 1) * 128] = o[low : low + 16]
 
 
-    rings = {"p": (0, 0, 1), "q": (1, 0, 0), "r": (2, 1, 0)}
+    rings = {"p": (0, 0, 1), "q": (1, 0, 0), "r": (0, 1, 0)}
 
     def product(half, dy, dz):
         if "out" not in done:
@@ -403,14 +407,14 @@
 
     def d_cross(half):
         sent[half, 1, 0, group[0]] = ring_end(half, "p").astype(BF)
-        send(f"y{half}", sent.at[half, 1, 0, group[0]], got_z.at[half, 4, group[0]], z_far)
+        send(f"y{half}", sent.at[half, 1, 0, group[0]], got_z.at[half, 0, group[0]], z_far)
 
     def d_end(half, p):
         low = half * ROWS
         if p == 0:
             first = ring_end(half, "q")
             arrived(f"y{half}")
-            first = (first + got_z[half, 4, group[0]].astype(F32)).astype(BF)
+            first = (first + got_z[half, 0, group[0]].astype(F32)).astype(BF)
             out[0, low : low + ROWS] = first[0:ROWS]
             out[1, low : low + FIRST - ROWS] = first[ROWS:FIRST]
         else:
@@ -480,6 +484,12 @@
         lax.fori_loop(0, 8, away, 0)
         send("bias", bias_away, bias.at[1], twin)
         lax.fori_loop(0, 8, here, 0)
+        fetched("lengths", "frequency")
+        spots = jnp.transpose(jnp.broadcast_to(lengths[...].astype(F32), (128, 128)))[:, 0:64]
+        for p in range(2):
+            angles = (spots + float(p)) * frequency[...]
+            cosine[p] = jnp.cos(angles)
+            sine[p] = jnp.sin(angles)
 
     def exchange_end():
         arrived("pages")
@@ -488,132 +498,132 @@
             vals[u, :, 128:256] = jnp.ones((1024, 128), BF)
         for half in range(CHUNKS):
             value_new[half, :, 128:256] = jnp.ones((TREES * 32, 128), BF)
-        fetched("pages", "pages_away", "keys", "values", "cosine", "sine")
+        fetched("pages", "pages_away", "keys", "values")
         arrived("keys", "values", "bias")
 
     g_start(1, 1)
     squares_start()
+    exchange_start()
     g_start(1, 0)
-    exchange_start()
+    g_start(0, 1)
     visibility()
-    exchange_end()
     g_down(1, 1, 0)
     g_up(1, 1, 0)
+    g_z(1)
     squares_end()
+    multiply(1, 0, 0)
+    multiply(1, 1, 0)
     multiply(0, 0, 0)
-    g_start(0, 1)
-    multiply(1, 0, 0)
-    g_z(1)
-    multiply(1, 3, 0)
-    multiply(1, 1, 0)
     g_up(1, 0, 0)
+    g_far(1, "d")
+    g_far(1, "u")
     g_down(1, 0, 0)
-    g_far(1, "u")
-    g_far(1, "d")
     multiply(1, 0, 1)
     g_up(1, 0, 1)
     g_down(1, 0, 1)
     g_start(0, 0)
-    g_down(0, 1, 0)
+    g_up(0, 1, 0)
+    exchange_end()
+    multiply(1, 3, 1)
     multiply(1, 1, 1)
-    multiply(1, 3, 1)
+    multiply(1, 3, 0)
     multiply(1, 2, 0)
     multiply(1, 2, 1)
     project_end(1)
-    g_up(0, 1, 0)
+    g_down(0, 1, 0)
+    fresh_tokens(1)
     g_z(0)
+    block(1, 0, 0)
     multiply(0, 0, 1)
-    block(1, 0, 0)
     g_far(0, "u")
-    g_far(0, "d")
     g_up(0, 0, 0)
-    fresh_tokens(1)
-    g_down(0, 0, 0)
-    multiply(0, 3, 0)
     q_up(1)
     q_down(1)
+    g_far(0, "d")
+    g_down(0, 0, 0)
     multiply(0, 1, 0)
+    multiply(0, 3, 0)
     block(1, 3, 0)
     g_up(0, 0, 1)
+    q_z(1)
+    q_cross(1, "u")
+    g_down(0, 0, 1)
+    multiply(0, 3, 1)
+    q_cross(1, "d")
     multiply(0, 1, 1)
-    g_down(0, 0, 1)
+    block(1, 2, 0)
+    multiply(0, 2, 0)
     block(1, 0, 1)
-    q_cross(1, "d")
-    q_z(1)
-    multiply(0, 3, 1)
-    q_cross(1, "u")
-    multiply(0, 2, 0)
-    block(1, 1, 0)
     multiply(0, 2, 1)
     project_end(0)
-    block(1, 2, 0)
     block(1, 2, 1)
     block(1, 3, 1)
-    fresh_tokens(0)
+    block(1, 1, 0)
     q_up(0)
     q_down(0)
     block(1, 1, 1)
+    c_join(1, 0, 0)
+    c_join(1, 0, 1)
     c_join(1, 1, 0)
     block(0, 0, 1)
+    q_cross(0, "u")
     c_join(1, 1, 1)
-    q_cross(0, "u")
     q_z(0)
     q_cross(0, "d")
-    c_join(1, 0, 0)
-    c_join(1, 0, 1)
     block(0, 2, 0)
     plane_merge(1, 0)
+    block(0, 1, 0)
     plane_merge(1, 1)
-    block(0, 1, 0)
+    fresh_tokens(0)
     block(0, 2, 1)
+    last_merge(1, 0)
     block(0, 1, 1)
-    last_merge(1, 0)
     last_merge(1, 1)
     d_far(1, 1)
+    d_far(1, 0)
     d_near(1, 3, 1)
-    d_near(1, 1, 0)
     block(0, 3, 1)
     c_join(0, 1, 0)
+    c_join(0, 0, 0)
+    d_near(1, 1, 1)
     c_join(0, 1, 1)
-    d_far(1, 0)
-    c_join(0, 0, 0)
-    c_join(0, 0, 1)
-    d_near(1, 1, 1)
+    d_join(1, "p", 3)
+    d_near(1, 1, 0)
+    block(0, 3, 0)
     d_join(1, "p", 1)
     r_far(1)
-    d_join(1, "p", 3)
-    block(0, 3, 0)
+    d_near(1, 3, 0)
+    d_join(1, "q", 3)
     plane_merge(0, 0)
+    d_join(1, "q", 1)
+    c_join(0, 0, 1)
     plane_merge(0, 1)
-    d_near(1, 3, 0)
+    block(0, 0, 0)
+    d_own(1, 1)
+    r_near(1, 1)
+    d_own(1, 0)
     r_near(1, 3)
-    d_own(1, 0)
     d_join(1, "r", 3)
-    d_join(1, "q", 1)
-    r_near(1, 1)
-    d_own(1, 1)
-    d_join(1, "q", 3)
-    block(0, 0, 0)
+    last_merge(0, 0)
     d_cross(1)
-    last_merge(0, 0)
     d_join(1, "r", 1)
     last_merge(0, 1)
     d_own(0, 0)
     d_far(0, 1)
+    d_far(0, 0)
     d_near(0, 1, 1)
+    d_end(1, 1)
     d_near(0, 3, 1)
-    d_far(0, 0)
+    d_join(0, "p", 3)
+    d_end(1, 0)
     d_own(0, 1)
     d_join(0, "p", 1)
-    d_join(0, "p", 3)
     r_far(0)
     d_near(0, 3, 0)
     d_join(0, "q", 3)
     d_near(0, 1, 0)
-    d_end(1, 1)
     r_near(0, 1)
     d_cross(0)
-    d_end(1, 0)
     d_join(0, "r", 1)
     d_join(0, "q", 1)
     r_near(0, 3)
@@ -631,7 +641,7 @@
     trees, tile = (n, TREES, 128, 128), (8, 128)
     stat = (n,) + tile
     shapes = [
-        ((64, 128), BF), ((8, 1, 1024), F32), ((2, 128, 64), F32), ((2, 128, 64), F32),
+        ((64, 128), BF), ((8, 1, 1024), F32), ((1, 128), jnp.int32), ((1, 64), F32), ((2, 128, 64), F32), ((2, 128, 64), F32),
         (tile, jnp.int32), ((1, 2048), jnp.int32),
         ((n, 4, 2, 2 * r, 1024), BF), ((4, 2) + tile, F32), ((n, 2 * r, 128), F32), ((8, 1024, 768), BF),
         ((n, 2 * r, 768), F32), ((512, 8192), BF), ((256, 64, 128), BF), ((256, 64, 128), BF), ((128, 512), F32),
@@ -641,7 +651,7 @@
         ((2,) + trees, BF), ((2,) + stat, F32), ((2,) + stat, F32), ((2,) + trees, BF), ((2,) + stat, F32),
         (trees, BF), (stat, F32),
         ((TREES, 1024, 256), BF), ((n, 2 * r, 512), BF), ((n, 2, 4, 2 * r, 1024), BF),
-        ((n, 3, 3, 2 * r, 1024), BF), ((n, 5, 2 * r, 1024), BF),
+        ((n, 2, 3, 2 * r, 1024), BF), ((n, 4, 2 * r, 1024), BF),
     ]
     scratch = [pltpu.VMEM(*s) if s else pltpu.SMEM((2, 8, 128), jnp.int32) for s in shapes]
     return pl.pallas_call(
@@ -658,15 +668,6 @@
     )(*operands)
 
 
-def rope_tables(row_length):
-    spots = row_length[None, :] + jnp.arange(2, dtype=jnp.int32)[:, None]
-    ladder = jnp.arange(64, dtype=F32) * (2.0 / 128)
-    frequency = jnp.power(jnp.float32(ROPE_BASE), -ladder)
-    angles = spots.astype(F32)[..., None] * frequency
-    cosine, sine = jnp.cos(angles), jnp.sin(angles)
-    return cosine, sine
-
-
 def body(
     hidden,
     norm_gain,
@@ -681,10 +682,11 @@
     row_depth,
     row_length,
 ):
-    cosine, sine = rope_tables(row_length)
+    ladder = np.arange(64, dtype=np.float32) * np.float32(2.0 / 128)
+    frequency = jnp.asarray(np.power(np.float32(ROPE_BASE), -ladder)[None, :])
     pages, fill = jnp.transpose(tree_pages[0]), jnp.transpose(page_fill[0])
     return call(
-        hidden, norm_gain.reshape(64, 128), cosine, sine, pages, fill, row_depth, w_query, key_weight, value_weight, w_out,
+        hidden, norm_gain.reshape(64, 128), row_length[None, :], frequency, pages, fill, row_depth, w_query, key_weight, value_weight, w_out,
         key_cache.reshape(128, 64, 128), value_cache.reshape(128, 64, 128),
     )
 

time: 102 us -> 93.8 us (0.920)
  Pallas kernels: 97.6 us -> 91.8 us
  other arithmetic: 1.91 us -> 0 us
    pallas_call x1, Pallas kernels: 97.6 us -> 91.8 us  [call(): pl.pallas_call(kernel, out_shape=jax.ShapeDtypeStruct((2, 128, 1024), BF)...]
    sin x1 -> x0, other arithmetic: 1.23 us -> none  [rope_tables(): cosine, sine = (jnp.cos(angles), jnp.sin(angles))]
where the time goes in v6:
time: 93.8 us; the launch traced here: 93.6 us
  Pallas kernels  91.8 us (98%)
  local copies, waits for them, and re-layouts  1.87 us (2%)
    pallas_call x1, Pallas kernels, call(): pl.pallas_call(kernel, out_shape=jax.ShapeDtypeStruct((2, 128, 1024), BF)...  91.8 us

profile of v6, /device:TPU:0, one launch (start us, length us, event | category | flops | bytes accessed | tf_op | source)
XLA Modules:
  0.0 93.6 jit_solution(2690246192533122884)
XLA Ops:
  0.0 91.8 %shard_map.127 = bf16[2,128,1024]{2,1,0:T(8,128)(2,1)} custom-call(bf16[2,128,1024]{2,1,0:T(8,128)(2,1)} %hidden_hbm.1, bf16[64,128]{1,0:T(8,128)(2,1)} %bitcast.12, s32[1,128]{1,0:T(1,128)} %bitcast.15, f32[1,64]{1,0:T(1,128)} %constant.2.clone.frequency_hbm, s32[8,128]{1,0:T(8,128)} %bitcast.13, s32[8,128]{1,0:T(8,128)} %bitcast.14, s32[1,2048]{1,0:T(1,128)} %depth_hbm.1, ...), custom_call_target="tpu_custom_call" | custom-call | flops 15000000512 | bytes 31457280 | tf_op jit(solution)/shard_map/pallas_call | solution.py:657
  91.8 1.9 %copy.15 = bf16[2,128,1024]{2,1,0:T(8,128)(2,1)} copy(bf16[2,128,1024]{2,1,0:T(8,128)(2,1)} %shard_map.127) | data formatting | bytes 1048576

commit v7 on v6

--- a/solution.py
+++ b/solution.py
@@ -47,6 +47,11 @@
     x_up, x_down, z_near = (in_cache(1, 0), h), (in_cache(3, 0), h), (in_cache(0, 1), h)
     twin = (c + 1 - 2 * core, h)
 
+    barrier = pltpu.get_barrier_semaphore()
+    others = [(c, in_head(*spot)) for spot in SPOTS[1:]] + [x_up, x_down, z_near, twin]
+    for device in others:
+        pl.semaphore_signal(barrier, inc=1, device_id=device, device_id_type=MESH)
+
     loads = {}
 
     def load(name, src, dst):
@@ -67,19 +72,17 @@
     load("depth", depth_hbm, depth)
     load("lengths", lengths_hbm, lengths)
     load("frequency", frequency_hbm, frequency)
-    for number, spot in enumerate(ORDER):
-        rows = pl.ds(pl.multiple_of(in_head(*spot) * 1024, 1024), 1024)
-        load(("q", number), w_query.at[rows], weight.at[number, :, pl.ds(0, 512)])
-        load(("k", number), key_weight.at[rows], weight.at[number, :, pl.ds(512, 128)])
-        load(("v", number), value_weight.at[rows], weight.at[number, :, pl.ds(640, 128)])
-    load("keys", key_hbm, keys.at[pl.ds(0, 128)])
-    load("values", value_hbm, values.at[pl.ds(0, 128)])
-    load("out", w_out_hbm, w_out)
-
-    barrier = pltpu.get_barrier_semaphore()
-    others = [(c, in_head(*spot)) for spot in SPOTS[1:]] + [x_up, x_down, z_near, twin]
-    for device in others:
-        pl.semaphore_signal(barrier, inc=1, device_id=device, device_id_type=MESH)
+
+    def start_loads():
+        for number, spot in enumerate(ORDER):
+            rows = pl.ds(pl.multiple_of(in_head(*spot) * 1024, 1024), 1024)
+            load(("q", number), w_query.at[rows], weight.at[number, :, pl.ds(0, 512)])
+            load(("k", number), key_weight.at[rows], weight.at[number, :, pl.ds(512, 128)])
+            load(("v", number), value_weight.at[rows], weight.at[number, :, pl.ds(640, 128)])
+        load("keys", key_hbm, keys.at[pl.ds(0, 128)])
+        load("values", value_hbm, values.at[pl.ds(0, 128)])
+        load("out", w_out_hbm, w_out)
+
     pl.semaphore_wait(barrier, len(others))
 
     made = {}
@@ -505,6 +508,7 @@
     squares_start()
     exchange_start()
     g_start(1, 0)
+    start_loads()
     g_start(0, 1)
     visibility()
     g_down(1, 1, 0)

time: 93.8 us -> 94 us (level)
  no operation moved by 1% of the time
where the time goes in v7:
time: 94 us; the launch traced here: 93.9 us
  Pallas kernels  92 us (98%)
  local copies, waits for them, and re-layouts  1.87 us (2%)
    pallas_call x1, Pallas kernels, call(): pl.pallas_call(kernel, out_shape=jax.ShapeDtypeStruct((2, 128, 1024), BF)...  92 us

profile of v7, /device:TPU:0, one launch (start us, length us, event | category | flops | bytes accessed | tf_op | source)
XLA Modules:
  0.0 93.9 jit_solution(16548574364837900030)
XLA Ops:
  0.0 92.0 %shard_map.127 = bf16[2,128,1024]{2,1,0:T(8,128)(2,1)} custom-call(bf16[2,128,1024]{2,1,0:T(8,128)(2,1)} %hidden_hbm.1, bf16[64,128]{1,0:T(8,128)(2,1)} %bitcast.12, s32[1,128]{1,0:T(1,128)} %bitcast.15, f32[1,64]{1,0:T(1,128)} %constant.2.clone.frequency_hbm, s32[8,128]{1,0:T(8,128)} %bitcast.13, s32[8,128]{1,0:T(8,128)} %bitcast.14, s32[1,2048]{1,0:T(1,128)} %depth_hbm.1, ...), custom_call_target="tpu_custom_call" | custom-call | flops 15000000512 | bytes 31457280 | tf_op jit(solution)/shard_map/pallas_call | solution.py:661
  92.0 1.9 %copy.15 = bf16[2,128,1024]{2,1,0:T(8,128)(2,1)} copy(bf16[2,128,1024]{2,1,0:T(8,128)(2,1)} %shard_map.127) | data formatting | bytes 1048576
